TPU v7x, 32 devices: a whole 2x2x4 slice. The times are simulated.
32 devices in a mesh: docs: 8 (over z, y), rep: 4 (over x, core).
Axes of the slice: x: 2, y: 2, z: 4, core: 2. Of those that a mesh axis runs over, the one named last changes fastest.
Arguments:
- queries: bfloat16 [4096, 1024], P(('docs', 'rep')), may hold values from -6 to 6
- adapter: bfloat16 [1024, 1024], replicated, may hold values from -0.1875 to 0.1875
- doc_table: bfloat16 [8192, 1024], P(('docs', 'rep')), may hold values from -6 to 6
- routes: int32 [4096, 4], P(('docs', 'rep')), may hold values from 0 to 31, all different within a row; in each aligned block of 128 rows (0 to 127, 128 to 255, ...) at most 32 rows name the same one
- doc_rows: int32 [4096, 4, 16], P(('docs', 'rep')), may hold values from 0 to 255, as said below
- labels: int32 [4096, 4, 16], P(('docs', 'rep')), may hold values from 0 to 4
Outputs:
- losses: float32 [4096], P(('docs', 'rep'))
- query_grads: bfloat16 [4096, 1024], P(('docs', 'rep'))
- adapter_grad: bfloat16 [1024, 1024], P('docs')
Inputs may be any that keep to these rules, and one draw needn't show every extreme that they name: `routes`: each query names 4 different owners; among the queries of one device no owner is named more than 32 times, and in every draw some owner is named exactly 32 times by some device's queries. `doc_rows`: the 16 rows of one query at one owner are distinct.
All inputs are finite; a program needn't handle non-finite values.
Results may differ from a plain program's by a relative error of at most 0.024.
Values may be sent and summed in bfloat16 or wider, within the bound.
A program may use at most 128 MiB of HBM per device.

v0:
```python
import math

import jax
import jax.numpy as jnp
from jax import lax
from jax.sharding import PartitionSpec as P

EPSILON = 1e-06
LOSS_SCALE = 128.0


def unit_rows(rows):
    widened = rows.astype(jnp.float32)
    return (
        widened / jnp.sqrt(jnp.mean(widened * widened, axis=-1, keepdims=True) + EPSILON)
    ).astype(jnp.bfloat16)


def on_device(queries, adapter, doc_table, routes, doc_rows, labels):
    doc_groups = lax.axis_size("docs")
    rep_groups = lax.axis_size("rep")
    devices = doc_groups * rep_groups
    query_rows, feature_width = queries.shape
    fanout = routes.shape[1]
    per_owner = doc_rows.shape[2]
    doc_count = doc_table.shape[0]
    capacity = max(2, 2 * query_rows * fanout // devices)
    slots_all = devices * capacity
    score_scale = 2.0 / math.sqrt(feature_width)
    adapted = jnp.dot(queries, adapter, preferred_element_type=jnp.float32)
    radius = jnp.sqrt(jnp.mean(adapted * adapted, axis=-1, keepdims=True) + EPSILON)
    unit_exact = adapted / radius
    unit_query = unit_exact.astype(jnp.bfloat16)
    owner_hits = (routes[:, :, None] == jnp.arange(devices, dtype=jnp.int32)[None, None, :]).astype(
        jnp.int32
    )
    per_query = jnp.sum(owner_hits, axis=1)
    row_index = jnp.arange(query_rows, dtype=jnp.int32)
    lower_table = (row_index[:, None] > row_index[None, :]).astype(jnp.float32)
    earlier = jnp.dot(
        lower_table, per_query.astype(jnp.float32), precision=lax.Precision.HIGHEST
    ).astype(jnp.int32)
    slot_index = jnp.sum(earlier[:, None, :] * owner_hits, axis=-1)
    placed = routes * capacity + slot_index
    target_slot = placed.reshape(-1)
    repeated = jnp.broadcast_to(
        unit_query[:, None, :], (query_rows, fanout, feature_width)
    ).reshape(-1, feature_width)
    outgoing = jnp.zeros((slots_all, feature_width), jnp.bfloat16).at[target_slot].set(repeated)
    outgoing_ids = (
        jnp.zeros((slots_all, per_owner), jnp.int32)
        .at[target_slot]
        .set(doc_rows.reshape(-1, per_owner))
    )
    outgoing = outgoing.reshape(doc_groups, rep_groups, capacity, feature_width)
    outgoing_ids = outgoing_ids.reshape(doc_groups, rep_groups, capacity, per_owner)
    arrived, arrived_ids = (
        lax.all_to_all(
            lax.all_to_all(outgoing, "docs", split_axis=0, concat_axis=0, tiled=True),
            "rep",
            split_axis=1,
            concat_axis=1,
            tiled=True,
        ),
        lax.all_to_all(
            lax.all_to_all(outgoing_ids, "docs", split_axis=0, concat_axis=0, tiled=True),
            "rep",
            split_axis=1,
            concat_axis=1,
            tiled=True,
        ),
    )
    arrived = arrived.reshape(slots_all, feature_width)
    arrived_ids = arrived_ids.reshape(slots_all, per_owner)
    doc_unit = unit_rows(doc_table)
    block_scores = lax.dot_general(
        arrived, doc_unit, (((1,), (1,)), ((), ())), preferred_element_type=jnp.float32
    )
    scores_out = jnp.take_along_axis(block_scores, arrived_ids, axis=1) * score_scale
    returned = lax.all_to_all(
        lax.all_to_all(
            scores_out.reshape(doc_groups, rep_groups, capacity, per_owner).astype(jnp.bfloat16),
            "docs",
            split_axis=0,
            concat_axis=0,
            tiled=True,
        ),
        "rep",
        split_axis=1,
        concat_axis=1,
        tiled=True,
    ).astype(jnp.float32)
    scores = returned.reshape(slots_all, per_owner)[placed]
    raised = jnp.exp(scores)
    norm_total = jnp.sum(raised, axis=(1, 2))
    label_weight = jnp.exp(labels.astype(jnp.float32))
    target = label_weight / jnp.sum(label_weight, axis=(1, 2), keepdims=True)
    losses = jnp.log(norm_total) - jnp.sum(target * scores, axis=(1, 2))
    weights = (LOSS_SCALE * (raised / norm_total[:, None, None] - target)).astype(jnp.bfloat16)
    weight_slots = (
        jnp.zeros((slots_all, per_owner), jnp.bfloat16)
        .at[target_slot]
        .set(weights.reshape(-1, per_owner))
    )
    weights_in = lax.all_to_all(
        lax.all_to_all(
            weight_slots.reshape(doc_groups, rep_groups, capacity, per_owner),
            "docs",
            split_axis=0,
            concat_axis=0,
            tiled=True,
        ),
        "rep",
        split_axis=1,
        concat_axis=1,
        tiled=True,
    )
    weights_in = weights_in.reshape(slots_all, per_owner)
    spread = (
        jnp.zeros((slots_all, doc_count), jnp.bfloat16)
        .at[jnp.arange(slots_all)[:, None], arrived_ids]
        .set(weights_in)
    )
    pull_out = (jnp.dot(spread, doc_unit, preferred_element_type=jnp.float32) * score_scale).astype(
        jnp.bfloat16
    )
    pull_out = pull_out.reshape(doc_groups, rep_groups, capacity, feature_width)
    pull_back = lax.all_to_all(
        lax.all_to_all(pull_out, "docs", split_axis=0, concat_axis=0, tiled=True),
        "rep",
        split_axis=1,
        concat_axis=1,
        tiled=True,
    )
    pull_rows = pull_back.reshape(slots_all, feature_width)[placed]
    pull_total = jnp.sum(pull_rows.astype(jnp.float32), axis=1)
    projection = jnp.mean(unit_exact * pull_total, axis=-1, keepdims=True)
    adapted_grad = ((pull_total - unit_exact * projection) / radius).astype(jnp.bfloat16)
    query_grads = lax.dot_general(
        adapted_grad, adapter, (((1,), (1,)), ((), ())), preferred_element_type=jnp.float32
    ).astype(jnp.bfloat16)
    inverse_root = 1.0 / math.sqrt(query_rows * devices)
    local_terms = lax.dot_general(
        queries, adapted_grad, (((0,), (0,)), ((), ())), preferred_element_type=jnp.float32
    )
    group_terms = lax.psum(local_terms.astype(jnp.bfloat16), "rep").astype(jnp.float32)
    summed = lax.psum_scatter(group_terms, "docs", scatter_dimension=0, tiled=True)
    adapter_grad = (summed * inverse_root).astype(jnp.bfloat16)
    return (losses, query_grads, adapter_grad)


def solution(mesh):
    placed = (
        P(("docs", "rep"), None),
        P(),
        P(("docs", "rep"), None),
        P(("docs", "rep"), None),
        P(("docs", "rep"), None, None),
        P(("docs", "rep"), None, None),
    )
    return jax.shard_map(
        on_device,
        mesh=mesh,
        in_specs=placed,
        out_specs=(P(("docs", "rep")), P(("docs", "rep"), None), P("docs", None)),
        check_vma=False,
    )
```

profile of v0, /device:TPU:0, one launch (start us, length us, event | category | flops | bytes accessed | tf_op | source)
XLA Modules:
  0.0 656.1 jit_solution(11197126531774181532)
XLA Ops:
  13.6 7.3 %all-to-all-start = ((s32[8,1,2048]{2,1,0:T(1,128)}), s32[8,1,2048]{2,1,0:T(1,128)S(1)}, u32[]{:S(2)}, u32[]{:S(2)}) async-start(s32[8,1,2048]{2,1,0:T(1,128)} %reshape.228), calls=%async_computation | async-start | bytes 131072 | tf_op jit(solution)/shard_map/all_to_all | solution.py:66
  23.8 4.8 scatter_custom_fusion.1
  28.6 6.0 all-to-all-start.2
  36.9 45.5 %all-to-all-done.2 = bf16[8,4,32,1024]{3,2,1,0:T(8,128)(2,1)} async-done(((bf16[8,4,32,1024]{3,2,1,0:T(8,128)(2,1)}), bf16[8,4,32,1024]{3,2,1,0:T(8,128)(2,1)}, u32[]{:S(2)}, u32[]{:S(2)}) %all-to-all-start.2) | async-done | bytes 2097184 | tf_op jit(solution)/shard_map/all_to_all | solution.py:59
  82.4 3.3 all-to-all-start.1
  85.7 3.2 copy.162
  89.8 4.4 all-to-all-start.3
  98.2 21.8 %all-to-all-done.3 = bf16[8,4,32,1024]{3,2,0,1:T(8,128)(2,1)} async-done(((bf16[8,4,32,1024]{3,2,0,1:T(8,128)(2,1)}), bf16[8,4,32,1024]{3,2,0,1:T(8,128)(2,1)}, u32[]{:S(2)}, u32[]{:S(2)}) %all-to-all-start.3) | async-done | bytes 2097184 | tf_op jit(solution)/shard_map/all_to_all | solution.py:58
  122.7 129.5 %gather_fusion.2 = f32[16384]{0:T(1024)S(1)} fusion(f32[1024,256]{1,0:T(8,128)S(1)} %fusion.15, s32[16384]{0:T(1024)S(1)} %reshape.177), kind=kCustom, calls=%fused_computation.2 | custom fusion | bytes 262144 | tf_op jit(solution)/shard_map/jit(take_along_axis)/gather | solution.py:79
  253.5 3.6 all-to-all-start.4
  257.2 6.7 %all-to-all-done.4 = bf16[8,2,1024]{2,1,0:T(2,128)(2,1)S(1)} async-done(((bf16[8,2,1024]{2,1,0:T(2,128)(2,1)}), bf16[8,2,1024]{2,1,0:T(2,128)(2,1)S(1)}, u32[]{:S(2)}, u32[]{:S(2)}) %all-to-all-start.4) | async-done | bytes 32800 | tf_op jit(solution)/shard_map/all_to_all | solution.py:81
  264.8 3.4 all-to-all-start.5
  268.4 3.6 all-to-all-done.5
  276.5 3.3 all-to-all-start.6
  280.0 6.5 all-to-all-done.6
  287.5 3.3 all-to-all-start.7
  291.2 3.4 all-to-all-done.7
  295.2 112.7 %scatter_custom_fusion.3 = bf16[262144]{0:T(1024)(128)(2,1)S(1)} fusion(s32[16384]{0:T(1024)S(1)} %reshape.207, bf16[16384]{0:T(1024)(128)(2,1)S(1)} %reshape.209, bf16[]{:T(256)} %constant.18.clone.1), kind=kCustom, calls=%fused_computation.22 | custom fusion | bytes 524290
  410.7 50.8 %all_to_all.50 = bf16[8,4,32,1024]{3,2,1,0:T(8,128)(2,1)S(1)} all-to-all(bf16[8,4,32,1024]{3,2,1,0:T(8,128)(2,1)S(1)} %bitcast.58), channel_id=1, replica_groups=mesh['docs'=8,'rep'=4] {'docs'}, dimensions={0} | all-to-all | bytes 4194304 | tf_op jit(solution)/shard_map/all_to_all | solution.py:129
  461.8 28.2 %all_to_all.51 = bf16[8,4,32,1024]{3,2,0,1:T(8,128)(2,1)S(1)} all-to-all(bf16[8,4,32,1024]{3,2,0,1:T(8,128)(2,1)S(1)} %copy.178), channel_id=1, replica_groups=mesh['docs'=8,'rep'=4] {'rep'}, dimensions={1} | all-to-all | bytes 4194304 | tf_op jit(solution)/shard_map/all_to_all | solution.py:128
  491.5 5.3 gather_fusion.1
  505.0 49.6 %all-reduce.2.cloned.1.call-done = bf16[1024,1024]{0,1:T(8,128)(2,1)} async-done(((bf16[1024,1024]{0,1:T(8,128)(2,1)}), bf16[1024,1024]{0,1:T(8,128)(2,1)}) %all-reduce.2.cloned.1.call-update) | async-done | bytes 2097168 | tf_op jit(solution)/shard_map/psum | solution.py:146
  554.6 4.0 convert_element_type.68
  560.7 86.6 %reduce-scatter.2.cloned.1.call-done = f32[128,1024]{0,1:T(8,128)} async-done(((f32[1024,1024]{0,1:T(8,128)}), f32[128,1024]{0,1:T(8,128)}) %reduce-scatter.2.cloned.1.call-update) | async-done | bytes 524304 | tf_op jit(solution)/shard_map/reduce_scatter | solution.py:147
  (128 shorter events, 44.5 us)
Async XLA Ops:
  7.2 13.7 %copy-start = (bf16[1024,1024]{1,0:T(8,128)(2,1)S(1)}, bf16[1024,1024]{1,0:T(8,128)(2,1)}, u32[]{:S(2)}) copy-start(bf16[1024,1024]{1,0:T(8,128)(2,1)} %param.7) | copy-start | bytes 6291460
  7.2 13.7 %copy-start.11 = (bf16[128,1024]{1,0:T(8,128)(2,1)S(1)}, bf16[128,1024]{1,0:T(8,128)(2,1)}, u32[]{:S(2)}) copy-start(bf16[128,1024]{1,0:T(8,128)(2,1)} %param.6) | copy-start | bytes 786436
  9.9 13.9 %copy-start.17 = (s32[512,1]{0,1:T(1,128)}, s32[512,1]{0,1:T(1,128)S(1)}, u32[]{:S(2)}) copy-start(s32[512,1]{0,1:T(1,128)S(1)} %compare_select_fusion.2) | copy-start | bytes 6148
  13.6 15.0 %all-to-all-start = ((s32[8,1,2048]{2,1,0:T(1,128)}), s32[8,1,2048]{2,1,0:T(1,128)S(1)}, u32[]{:S(2)}, u32[]{:S(2)}) async-start(s32[8,1,2048]{2,1,0:T(1,128)} %reshape.228), calls=%async_computation | async-start | bytes 131072 | tf_op jit(solution)/shard_map/all_to_all | solution.py:66
  28.6 53.8 %all-to-all-start.2 = ((bf16[8,4,32,1024]{3,2,1,0:T(8,128)(2,1)}), bf16[8,4,32,1024]{3,2,1,0:T(8,128)(2,1)}, u32[]{:S(2)}, u32[]{:S(2)}) async-start(bf16[8,4,32,1024]{3,2,1,0:T(8,128)(2,1)} %bitcast.55), calls=%async_computation.2 | async-start | bytes 4194304 | tf_op jit(solution)/shard_map/all_to_all | solution.py:59
  82.4 7.4 %all-to-all-start.1 = ((s32[4,1,4096]{2,1,0:T(1,128)}), s32[4,1,4096]{2,1,0:T(1,128)S(1)}, u32[]{:S(2)}, u32[]{:S(2)}) async-start(s32[4,1,4096]{2,1,0:T(1,128)} %reshape.230), calls=%async_computation.1 | async-start | bytes 131072 | tf_op jit(solution)/shard_map/all_to_all | solution.py:65
  88.9 6.1 copy-start.9
  88.9 6.7 %copy-start.6 = (bf16[256,1024]{1,0:T(8,128)(2,1)S(1)}, bf16[256,1024]{1,0:T(8,128)(2,1)}, u32[]{:S(2)}) copy-start(bf16[256,1024]{1,0:T(8,128)(2,1)} %param.8) | copy-start | bytes 1572868
  89.8 30.2 %all-to-all-start.3 = ((bf16[8,4,32,1024]{3,2,0,1:T(8,128)(2,1)}), bf16[8,4,32,1024]{3,2,0,1:T(8,128)(2,1)}, u32[]{:S(2)}, u32[]{:S(2)}) async-start(bf16[8,4,32,1024]{3,2,0,1:T(8,128)(2,1)} %copy.162), calls=%async_computation.3 | async-start | bytes 4194304 | tf_op jit(solution)/shard_map/all_to_all | solution.py:58
  95.8 26.0 %copy-start.18 = (f32[256]{0:T(256)}, f32[256]{0:T(256)S(1)}, u32[]{:S(2)}) copy-start(f32[256]{0:T(256)S(1)} %add_sqrt_fusion) | copy-start | bytes 3076
  122.7 129.9 %copy-start.4 = (s32[4,8,16,32]{3,2,1,0:T(8,128)S(1)}, s32[4,8,16,32]{3,2,1,0:T(8,128)}, u32[]{:S(2)}) copy-start(s32[4,8,16,32]{3,2,1,0:T(8,128)} %copy-done.3) | copy-start | bytes 196612
  252.2 16.0 %copy-start.5 = (s32[1024,16,1]{0,1,2:T(8,128)S(1)}, s32[1024,16,1]{0,1,2:T(8,128)}, u32[]{:S(2)}) copy-start(s32[1024,16,1]{0,1,2:T(8,128)} %get-tuple-element.31) | copy-start | bytes 196612
  252.2 16.0 %copy-start.21 = (s32[2]{0:T(128)S(1)}, s32[2]{0:T(128)}, u32[]{:S(2)}) copy-start(s32[2]{0:T(128)} %constant.27) | copy-start | bytes 28
  253.5 10.3 %all-to-all-start.4 = ((bf16[8,2,1024]{2,1,0:T(2,128)(2,1)}), bf16[8,2,1024]{2,1,0:T(2,128)(2,1)S(1)}, u32[]{:S(2)}, u32[]{:S(2)}) async-start(bf16[8,2,1024]{2,1,0:T(2,128)(2,1)} %reshape.232), calls=%async_computation.4 | async-start | bytes 65536 | tf_op jit(solution)/shard_map/all_to_all | solution.py:81
  264.0 9.4 %copy-start.10 = (s32[128,4,16]{0,2,1:T(8,128)S(1)}, s32[128,4,16]{0,2,1:T(8,128)}, u32[]{:S(2)}) copy-start(s32[128,4,16]{0,2,1:T(8,128)} %param.11) | copy-start | bytes 98308
  264.0 9.4 %copy-start.14 = (f32[128]{0:T(128)S(1)}, f32[128]{0:T(128)}, u32[]{:S(2)}) copy-start(f32[128]{0:T(128)} %fusion.11) | copy-start | bytes 1540
  264.8 7.2 %all-to-all-start.5 = ((bf16[4,2,2048]{2,1,0:T(2,128)(2,1)}), bf16[4,2,2048]{2,1,0:T(2,128)(2,1)S(1)}, u32[]{:S(2)}, u32[]{:S(2)}) async-start(bf16[4,2,2048]{2,1,0:T(2,128)(2,1)} %reshape.234), calls=%async_computation.5 | async-start | bytes 65536 | tf_op jit(solution)/shard_map/all_to_all | solution.py:80
  272.3 7.6 %copy-start.20 = (s32[2]{0:T(128)S(1)}, s32[2]{0:T(128)}, u32[]{:S(2)}) copy-start(s32[2]{0:T(128)} %constant.11) | copy-start | bytes 28
  276.5 10.0 %all-to-all-start.6 = ((bf16[8,2,1024]{2,1,0:T(2,128)(2,1)}), bf16[8,2,1024]{2,1,0:T(2,128)(2,1)S(1)}, u32[]{:S(2)}, u32[]{:S(2)}) async-start(bf16[8,2,1024]{2,1,0:T(2,128)(2,1)} %reshape.236), calls=%async_computation.6 | async-start | bytes 65536 | tf_op jit(solution)/shard_map/all_to_all | solution.py:106
  286.6 122.2 %copy-start.8 = (bf16[256,1024]{1,0:T(8,128)(2,1)S(1)}, bf16[256,1024]{1,0:T(8,128)(2,1)}, u32[]{:S(2)}) copy-start(bf16[256,1024]{1,0:T(8,128)(2,1)} %param.8) | copy-start | bytes 1572868
  286.7 122.2 %copy-start.19 = (f32[256]{0:T(256)S(1)}, f32[256]{0:T(256)}, u32[]{:S(2)}) copy-start(f32[256]{0:T(256)} %copy-done.18) | copy-start | bytes 3076
  287.5 7.2 %all-to-all-start.7 = ((bf16[4,2,2048]{2,1,0:T(2,128)(2,1)}), bf16[4,2,2048]{2,1,0:T(2,128)(2,1)S(1)}, u32[]{:S(2)}, u32[]{:S(2)}) async-start(bf16[4,2,2048]{2,1,0:T(2,128)(2,1)} %reshape.238), calls=%async_computation.7 | async-start | bytes 65536 | tf_op jit(solution)/shard_map/all_to_all | solution.py:105
  290.7 263.8 %all-reduce.2.cloned.1.call-start = ((), (), s32[]{:S(2)}) async-start(), calls=%async_computation.11 | async-start | bytes 4194304 | tf_op jit(solution)/shard_map/psum | solution.py:146
  504.9 142.4 %reduce-scatter.2.cloned.1.call-start = ((), (), s32[]{:S(2)}) async-start(), calls=%async_computation.12 | async-start | bytes 4718592 | tf_op jit(solution)/shard_map/reduce_scatter | solution.py:147
  (8 other events, 18.5 us)
Sparse Core Ops, SparseCore 0:
  505.1 49.4 all-reduce.1
  558.7 88.5 reduce-scatter.1
where the time goes:
time: 657 us; the launch traced here: 656 us
  local copies, waits for them, and re-layouts  281 us (43%)
  waiting for transfers between devices  225 us (34%)
  blocking collectives  79 us (12%)
  starting transfers between devices  34.8 us (5%)
  between operations  14.6 us (2%)
  other arithmetic  14.5 us (2%)
  matrix products  7.12 us (1%)
    gather x6, local copies, waits for them, and re-layouts, on_device(): jnp.take_along_axis(block_scores, arrived_ids, axis=1) * score_scale  130 us
    unnamed x64, local copies, waits for them, and re-layouts  121 us
    reduce_scatter x1, waiting for transfers between devices, on_device(): lax.psum_scatter(group_terms, 'docs', scatter_dimension=0, tiled=True)  86.6 us
    all_to_all x1, blocking collectives, on_device(): lax.all_to_all(pull_out, 'docs', split_axis=0, concat_axis=0, tiled=True)  50.8 us
    psum x1, waiting for transfers between devices, on_device(): lax.psum(local_terms.astype(jnp.bfloat16), 'rep').astype(jnp.float32)  49.6 us
    all_to_all x1, waiting for transfers between devices, on_device(): lax.all_to_all(outgoing, 'docs', split_axis=0, concat_axis=0, tiled=True)  45.5 us
    all_to_all x1, blocking collectives, on_device(): lax.all_to_all(lax.all_to_all(pull_out, 'docs', split_axis=0, concat_axis...  28.2 us
    all_to_all x1, waiting for transfers between devices, on_device(): lax.all_to_all(lax.all_to_all(outgoing, 'docs', split_axis=0, concat_axis...  21.8 us
  transfers between devices with their start and end apart: 10, of which 9 were waited for; matrix products, arithmetic and copies ran while one was open for 3% of the time, Pallas kernels for 0%

commit v1 on v0

--- a/solution.py
+++ b/solution.py
@@ -1,12 +1,17 @@
+import functools
 import math
 
 import jax
 import jax.numpy as jnp
 from jax import lax
+from jax.experimental import pallas as pl
+from jax.experimental.pallas import tpu as pltpu
 from jax.sharding import PartitionSpec as P
 
 EPSILON = 1e-06
 LOSS_SCALE = 128.0
+MESH = pl.DeviceIdType.MESH
+GATHER_LIMIT = 8 * 1024 * 1024
 
 
 def unit_rows(rows):
@@ -16,7 +21,7 @@
     ).astype(jnp.bfloat16)
 
 
-def on_device(queries, adapter, doc_table, routes, doc_rows, labels):
+def routed_on_device(queries, adapter, doc_table, routes, doc_rows, labels):
     doc_groups = lax.axis_size("docs")
     rep_groups = lax.axis_size("rep")
     devices = doc_groups * rep_groups
@@ -149,6 +154,393 @@
     return (losses, query_grads, adapter_grad)
 
 
+def dot_nt(a, b):
+    return lax.dot_general(a, b, (((1,), (1,)), ((), ())), preferred_element_type=jnp.float32)
+
+
+def dot_tn(a, b):
+    return lax.dot_general(a, b, (((0,), (0,)), ((), ())), preferred_element_type=jnp.float32)
+
+
+def ring_group(position, groups):
+    column = position // (groups // 2)
+    along = position + column * (groups - 1 - 2 * position)
+    return 2 * along + column
+
+
+def gathered_kernel(
+    groups, reps, fanout, per_owner, inverse_root,
+    queries_ref, adapter_ref, doc_ref, meta_ref,
+    loss_ref, query_grad_ref, adapter_grad_ref,
+    docs_all, unit_all, raw_all, meta_all, unit_exact_ref, radius_ref,
+    raised_all, target_all, score_ref, label_sum, stats, stats_in, weight_ref,
+    pull_out, pull_in, grad_cols, grad_in, terms_out, terms_in, final_cols,
+    ring_send, ring_recv, rep_send, rep_recv, small_send, small_recv,
+    terms_send, terms_recv,
+):
+    docs_at = lax.axis_index("docs")
+    rep_at = lax.axis_index("rep")
+    rows, width = queries_ref.shape
+    doc_count = doc_ref.shape[0]
+    half = doc_count // 2
+    others = reps - 1
+    candidates = fanout * per_owner
+    score_scale = 2.0 / math.sqrt(width)
+
+    def rep_peer(step):
+        return lax.rem(rep_at + step, reps)
+
+    along, column = docs_at // 2, docs_at % 2
+    place = along + column * (groups - 1 - 2 * along)
+    right = ring_group(lax.rem(place + 1, groups), groups)
+    left = ring_group(lax.rem(place + groups - 1, groups), groups)
+
+    barrier = pltpu.get_barrier_semaphore()
+    for step in range(1, reps):
+        pl.semaphore_signal(
+            barrier, inc=1, device_id=(docs_at, rep_peer(step)), device_id_type=MESH
+        )
+    for step in range(1, groups):
+        pl.semaphore_signal(
+            barrier, inc=1, device_id=(lax.rem(docs_at + step, groups), rep_at), device_id_type=MESH
+        )
+    docs_all[0] = unit_rows(doc_ref[...])
+    pl.semaphore_wait(barrier, others + groups - 1)
+
+    def ring_copy(way, index):
+        hop = index // 2
+        if way == 0:
+            part, source, landing, device = index % 2, hop, hop + 1, right
+        else:
+            part, source, landing, device = (
+                1 - index % 2, (groups - hop) % groups, groups - hop - 1, left
+            )
+        return pltpu.make_async_remote_copy(
+            src_ref=docs_all.at[source, pl.ds(part * half, half)],
+            dst_ref=docs_all.at[landing, pl.ds(part * half, half)],
+            send_sem=ring_send.at[way, index],
+            recv_sem=ring_recv.at[way, index],
+            device_id=(device, rep_at),
+            device_id_type=MESH,
+        )
+
+    ring_steps = groups - 1
+    for index in range(2):
+        for way in range(2):
+            ring_copy(way, index).start()
+
+    def rep_copy(kind, at, source, landing):
+        return pltpu.make_async_remote_copy(
+            src_ref=source,
+            dst_ref=landing,
+            send_sem=rep_send.at[kind, at],
+            recv_sem=rep_recv.at[kind, at],
+            device_id=(docs_at, rep_peer(at + 1)),
+            device_id_type=MESH,
+        )
+
+    meta_copies = [rep_copy(0, at, meta_ref, meta_all.at[at]) for at in range(others)]
+    for copy in meta_copies:
+        copy.start()
+    adapted = jnp.dot(queries_ref[...], adapter_ref[...], preferred_element_type=jnp.float32)
+    radius = jnp.sqrt(jnp.mean(adapted * adapted, axis=-1, keepdims=True) + EPSILON)
+    unit_exact = adapted / radius
+    unit_exact_ref[...] = unit_exact
+    radius_ref[...] = radius
+    unit_all[others] = unit_exact.astype(jnp.bfloat16)
+    unit_copies = [rep_copy(1, at, unit_all.at[others], unit_all.at[at]) for at in range(others)]
+    for copy in unit_copies:
+        copy.start()
+    raw_copies = [rep_copy(2, at, queries_ref, raw_all.at[at]) for at in range(others)]
+    for copy in raw_copies:
+        copy.start()
+    raw_all[others] = queries_ref[...]
+    meta_all[others] = meta_ref[...]
+    stats[...] = jnp.zeros_like(stats)
+
+    tile = 64
+    tiles = doc_count // tile
+
+    def label_mask(slot):
+        owner = ring_group(lax.rem(place + groups - slot, groups), groups) * reps + rep_at
+
+        def step(index, carry):
+            at = index // tiles
+            first = pl.multiple_of((index % tiles) * tile, tile)
+            lanes = pl.ds(pl.multiple_of(at * rows, rows), rows)
+            owners = meta_all[at, 2 * candidates : 2 * candidates + 8, :]
+            ids = jnp.full((per_owner, rows), -1, jnp.int32)
+            marks = jnp.zeros((per_owner, rows), jnp.int32)
+            for k in range(fanout):
+                named = owners[k : k + 1, :] == owner
+                ids = jnp.where(named, meta_all[at, k * per_owner : (k + 1) * per_owner, :], ids)
+                low = candidates + k * per_owner
+                marks = jnp.where(named, meta_all[at, low : low + per_owner, :] + 1, marks)
+            marks = marks.astype(jnp.float32)
+            here = lax.broadcasted_iota(jnp.int32, (tile, rows), 0) + first
+            found = jnp.zeros((tile, rows), jnp.float32)
+            for m in range(per_owner):
+                found = jnp.where(here == ids[m : m + 1, :], marks[m : m + 1, :], found)
+            target_all[slot, pl.ds(first, tile), lanes] = found
+            return carry
+
+        lax.fori_loop(0, reps * tiles, step, 0)
+
+    def score(slot):
+        score_ref[...] = (
+            dot_nt(docs_all[slot], unit_all[...].reshape(reps * rows, width)) * score_scale
+        )
+        for at in range(reps):
+            lanes = pl.ds(at * rows, rows)
+
+            def step(index, totals):
+                span = pl.ds(pl.multiple_of(index * tile, tile), tile)
+                marks = target_all[slot, span, lanes]
+                scores = score_ref[span, lanes]
+                held = marks > 0.5
+                raised = jnp.where(held, jnp.exp(scores), 0.0)
+                target = jnp.where(held, jnp.exp(marks - 1.0), 0.0) * label_sum[at, 0:1, :]
+                raised_all[slot, span, lanes] = raised
+                target_all[slot, span, lanes] = target * LOSS_SCALE
+                return (
+                    totals[0] + jnp.sum(raised, axis=0, keepdims=True),
+                    totals[1] + jnp.sum(target * scores, axis=0, keepdims=True),
+                )
+
+            zero = jnp.zeros((1, rows), jnp.float32)
+            norm, dotted = lax.fori_loop(0, tiles, step, (zero, zero))
+            stats[at, 0:1, :] += norm
+            stats[at, 1:2, :] += dotted
+
+    for index in range(ring_steps):
+        for way in range(2):
+            ring_copy(way, index).wait_recv()
+            if index + 2 < ring_steps:
+                ring_copy(way, index + 2).start()
+        if index == 0:
+            for copy in meta_copies:
+                copy.wait_recv()
+            for at in range(reps):
+                raised_labels = jnp.exp(
+                    meta_all[at, candidates : 2 * candidates, :].astype(jnp.float32)
+                )
+                label_sum[at, 0:1, :] = 1.0 / jnp.sum(raised_labels, axis=0, keepdims=True)
+            for slot in range(4):
+                label_mask(slot)
+        elif index == 1:
+            for slot in range(4, groups):
+                label_mask(slot)
+        elif index == 2:
+            for copy in unit_copies:
+                copy.wait_recv()
+            score(0)
+            score(1)
+            score(groups - 1)
+        elif index % 2 == 0:
+            score(index // 2)
+            score(groups - index // 2)
+    score(groups // 2)
+
+    def small_copy(kind, at, peer, source, landing):
+        return pltpu.make_async_remote_copy(
+            src_ref=source,
+            dst_ref=landing,
+            send_sem=small_send.at[kind, at],
+            recv_sem=small_recv.at[kind, at],
+            device_id=(docs_at, peer),
+            device_id_type=MESH,
+        )
+
+    stat_copies = [
+        small_copy(0, at, rep_peer(at + 1), stats, stats_in.at[at]) for at in range(others)
+    ]
+    for copy in stat_copies:
+        copy.start()
+    for copy in stat_copies:
+        copy.wait_recv()
+    norms = []
+    for at in range(reps):
+        total = stats[at]
+        for origin in range(others):
+            total = total + stats_in[origin, (at - origin - 1) % reps]
+        norms.append(total)
+    loss_ref[...] = jnp.log(norms[others][0:1, :]) - norms[others][1:2, :]
+
+    pull_copies = [
+        small_copy(1, at, rep_peer(reps - at - 1), pull_out.at[at], pull_in.at[at])
+        for at in range(others)
+    ]
+    all_docs = docs_all[...].reshape(groups * doc_count, width)
+    own_pull = None
+    for pair in range(reps // 2):
+        for at in (2 * pair, 2 * pair + 1):
+            share = LOSS_SCALE / norms[at][0:1, :]
+            lanes = pl.ds(at * rows, rows)
+
+            def weigh(slot, carry):
+                weight_ref[slot, :, lanes] = (
+                    raised_all[slot, :, lanes] * share - target_all[slot, :, lanes]
+                ).astype(jnp.bfloat16)
+                return carry
+
+            lax.fori_loop(0, groups, weigh, 0)
+        lanes = pl.ds(2 * pair * rows, 2 * rows)
+        pulled = (
+            dot_tn(weight_ref[:, :, lanes].reshape(groups * doc_count, 2 * rows), all_docs)
+            * score_scale
+        )
+        for at in (2 * pair, 2 * pair + 1):
+            low = (at - 2 * pair) * rows
+            if at < others:
+                pull_out[at] = pulled[low : low + rows].astype(jnp.bfloat16)
+                pull_copies[at].start()
+            else:
+                own_pull = pulled[low : low + rows]
+    pull_total = own_pull
+    for at in range(others):
+        pull_copies[at].wait_recv()
+        pull_total = pull_total + pull_in[at].astype(jnp.float32)
+    unit = unit_exact_ref[...]
+    projection = jnp.mean(unit * pull_total, axis=-1, keepdims=True)
+    adapted_grad = ((pull_total - unit * projection) / radius_ref[...]).astype(jnp.bfloat16)
+    block = width // reps
+    for at in range(reps):
+        grad_cols[at] = adapted_grad[:, at * block : (at + 1) * block]
+    grad_copies = [
+        small_copy(2, at, rep_peer(at + 1), grad_cols.at[rep_peer(at + 1)], grad_in.at[at])
+        for at in range(others)
+    ]
+    for copy in grad_copies:
+        copy.start()
+    grad_in[others] = grad_cols[rep_at]
+    query_grad_ref[...] = dot_nt(adapted_grad, adapter_ref[...]).astype(jnp.bfloat16)
+    for at in range(others):
+        raw_copies[at].wait_recv()
+        grad_copies[at].wait_recv()
+    group_terms = dot_tn(
+        raw_all[...].reshape(reps * rows, width), grad_in[...].reshape(reps * rows, block)
+    )
+    out_rows = width // groups
+    terms_out[...] = group_terms.astype(jnp.bfloat16).reshape(groups, out_rows, block)
+    term_copies = []
+    for step in range(1, groups):
+        peer = lax.rem(docs_at + step, groups)
+        copy = pltpu.make_async_remote_copy(
+            src_ref=terms_out.at[peer],
+            dst_ref=terms_in.at[step - 1],
+            send_sem=terms_send.at[step - 1],
+            recv_sem=terms_recv.at[step - 1],
+            device_id=(peer, rep_at),
+            device_id_type=MESH,
+        )
+        copy.start()
+        term_copies.append(copy)
+    summed = terms_out[docs_at].astype(jnp.float32)
+    for step in range(groups - 1):
+        term_copies[step].wait_recv()
+        summed = summed + terms_in[step].astype(jnp.float32)
+    final_cols[rep_at] = (summed * inverse_root).astype(jnp.bfloat16)
+    final_copies = [
+        small_copy(3, at, rep_peer(at + 1), final_cols.at[rep_at], final_cols.at[rep_at])
+        for at in range(others)
+    ]
+    for copy in final_copies:
+        copy.start()
+    for copy in final_copies:
+        copy.wait_recv()
+    for at in range(reps):
+        adapter_grad_ref[:, at * block : (at + 1) * block] = final_cols[at]
+
+    for index in range(ring_steps):
+        for way in range(2):
+            ring_copy(way, index).wait_send()
+    for copy in (
+        meta_copies + unit_copies + raw_copies + stat_copies + pull_copies
+        + grad_copies + term_copies + final_copies
+    ):
+        copy.wait_send()
+
+
+def gathered_on_device(queries, adapter, doc_table, routes, doc_rows, labels):
+    groups = lax.axis_size("docs")
+    reps = lax.axis_size("rep")
+    rows, width = queries.shape
+    fanout = routes.shape[1]
+    per_owner = doc_rows.shape[2]
+    doc_count = doc_table.shape[0]
+    candidates = fanout * per_owner
+    block = width // reps
+    out_rows = width // groups
+    others = reps - 1
+    meta = jnp.concatenate(
+        [
+            doc_rows.reshape(rows, candidates),
+            labels.reshape(rows, candidates),
+            routes,
+            jnp.zeros((rows, 8 - fanout), jnp.int32),
+        ],
+        axis=1,
+    ).T
+    meta_rows = meta.shape[0]
+    bf16, f32 = jnp.bfloat16, jnp.float32
+    vmem = pltpu.VMEM
+    dma = pltpu.SemaphoreType.DMA
+    losses, query_grads, adapter_grad = pl.pallas_call(
+        functools.partial(
+            gathered_kernel, groups, reps, fanout, per_owner,
+            1.0 / math.sqrt(rows * groups * reps),
+        ),
+        out_shape=(
+            jax.ShapeDtypeStruct((1, rows), f32),
+            jax.ShapeDtypeStruct((rows, width), bf16),
+            jax.ShapeDtypeStruct((out_rows, width), bf16),
+        ),
+        in_specs=[pl.BlockSpec(memory_space=vmem)] * 4,
+        out_specs=[pl.BlockSpec(memory_space=vmem)] * 3,
+        scratch_shapes=[
+            vmem((groups, doc_count, width), bf16),
+            vmem((reps, rows, width), bf16),
+            vmem((reps, rows, width), bf16),
+            vmem((reps, meta_rows, rows), jnp.int32),
+            vmem((rows, width), f32),
+            vmem((rows, 1), f32),
+            vmem((groups, doc_count, reps * rows), f32),
+            vmem((groups, doc_count, reps * rows), f32),
+            vmem((doc_count, reps * rows), f32),
+            vmem((reps, 8, rows), f32),
+            vmem((reps, 8, rows), f32),
+            vmem((others, reps, 8, rows), f32),
+            vmem((groups, doc_count, reps * rows), bf16),
+            vmem((others, rows, width), bf16),
+            vmem((others, rows, width), bf16),
+            vmem((reps, rows, block), bf16),
+            vmem((reps, rows, block), bf16),
+            vmem((groups, out_rows, block), bf16),
+            vmem((groups - 1, out_rows, block), bf16),
+            vmem((reps, out_rows, block), bf16),
+            dma((2, groups - 1)),
+            dma((2, groups - 1)),
+            dma((3, others)),
+            dma((3, others)),
+            dma((4, others)),
+            dma((4, others)),
+            dma((groups - 1,)),
+            dma((groups - 1,)),
+        ],
+        compiler_params=pltpu.CompilerParams(
+            collective_id=0, has_side_effects=True, vmem_limit_bytes=48 * 1024 * 1024
+        ),
+    )(queries, adapter, doc_table, meta)
+    return (losses.reshape(rows), query_grads, adapter_grad)
+
+
+def on_device(queries, adapter, doc_table, routes, doc_rows, labels):
+    gathered_bytes = lax.axis_size("docs") * doc_table.size * doc_table.dtype.itemsize
+    if gathered_bytes <= GATHER_LIMIT and lax.axis_size("rep") % 2 == 0:
+        return gathered_on_device(queries, adapter, doc_table, routes, doc_rows, labels)
+    return routed_on_device(queries, adapter, doc_table, routes, doc_rows, labels)
+
+
 def solution(mesh):
     placed = (
         P(("docs", "rep"), None),

time: 657 us -> 96.4 us (0.15)
  the two profiles are of different devices: /device:TPU:0 before, /device:TPU:15 now
where the time goes in v1:
time: 96.4 us; the launch traced here: 96.1 us
  Pallas kernels  89 us (92%)
  local copies, waits for them, and re-layouts  5.57 us (6%)
    pallas_call x1, Pallas kernels, gathered_on_device(): pl.pallas_call(functools.partial(gathered_kernel, groups, reps, fanout, p...  89 us
    unnamed x9, local copies, waits for them, and re-layouts  5.49 us

profile of v1, /device:TPU:15, one launch (start us, length us, event | category | flops | bytes accessed | tf_op | source)
XLA Modules:
  0.0 96.1 jit_solution(2883714698841319923)
XLA Ops:
  0.6 0.1 pad.3.clone
  0.7 0.9 add_bitcast_fusion.meta_ref
  1.6 0.0 copy-start
  1.6 1.6 %copy-done = bf16[1024,1024]{1,0:T(8,128)(2,1)S(1)} copy-done((bf16[1024,1024]{1,0:T(8,128)(2,1)S(1)}, bf16[1024,1024]{1,0:T(8,128)(2,1)}, u32[]{:S(2)}) %copy-start) | copy-done | bytes 2097176
  3.2 0.0 copy-start.1
  3.2 1.0 %copy-done.1 = bf16[256,1024]{1,0:T(8,128)(2,1)S(1)} copy-done((bf16[256,1024]{1,0:T(8,128)(2,1)S(1)}, bf16[256,1024]{1,0:T(8,128)(2,1)}, u32[]{:S(2)}) %copy-start.1) | copy-done | bytes 524312
  4.2 0.0 copy-start.2
  4.2 0.9 copy-done.2
  5.2 89.0 %shard_map.85 = (f32[1,128]{1,0:T(1,128)S(1)}, bf16[128,1024]{1,0:T(8,128)(2,1)S(1)}, bf16[128,1024]{1,0:T(8,128)(2,1)S(1)}) custom-call(bf16[128,1024]{1,0:T(8,128)(2,1)S(1)} %copy-done.2, bf16[1024,1024]{1,0:T(8,128)(2,1)S(1)} %copy-done, bf16[256,1024]{1,0:T(8,128)(2,1)S(1)} %copy-done.1, s32[136,128]{1,0:T(8,128)S(1)} %add_bitcast_fusion.meta_ref), custom_call_target="tpu_custom_call" | custom-call | tf_op jit(solution)/shard_map/pallas_call | solution.py:488
  94.2 0.5 copy.12
  94.7 0.7 copy.13
  95.4 0.7 copy.14
  (1 shorter events, 0.0 us)
Async XLA Ops:
  1.6 1.6 %copy-start = (bf16[1024,1024]{1,0:T(8,128)(2,1)S(1)}, bf16[1024,1024]{1,0:T(8,128)(2,1)}, u32[]{:S(2)}) copy-start(bf16[1024,1024]{1,0:T(8,128)(2,1)} %adapter_ref.1) | copy-start | bytes 6291460
  3.2 1.0 %copy-start.1 = (bf16[256,1024]{1,0:T(8,128)(2,1)S(1)}, bf16[256,1024]{1,0:T(8,128)(2,1)}, u32[]{:S(2)}) copy-start(bf16[256,1024]{1,0:T(8,128)(2,1)} %doc_ref.1) | copy-start | bytes 1572868
  4.2 0.9 copy-start.2

commit v2 on v1

--- a/solution.py
+++ b/solution.py
@@ -170,13 +170,15 @@
 
 def gathered_kernel(
     groups, reps, fanout, per_owner, inverse_root,
-    queries_ref, adapter_ref, doc_ref, meta_ref,
+    queries_ref, adapter_hbm, doc_hbm, routes_hbm, doc_rows_hbm, labels_hbm,
     loss_ref, query_grad_ref, adapter_grad_ref,
-    docs_all, unit_all, raw_all, meta_all, unit_exact_ref, radius_ref,
-    raised_all, target_all, score_ref, label_sum, stats, stats_in, weight_ref,
-    pull_out, pull_in, grad_cols, grad_in, terms_out, terms_in, final_cols,
-    ring_send, ring_recv, rep_send, rep_recv, small_send, small_recv,
-    terms_send, terms_recv,
+    adapter_ref, doc_ref, docs_all, unit_all, raw_all, meta_all, routes_all, radius_all,
+    marks_all, score_ref, weight_ref, sums, label_sum, stats, stats_in,
+    pair_out, pair_in, cross_out, cross_in, near_out, near_in, pull_ref,
+    project_out, project_in, grad_cols, grad_home,
+    terms_out, terms_in, final_cols,
+    load_sem, ring_send, ring_recv, rep_send, rep_recv, pull_send, pull_recv,
+    terms_send, terms_recv, final_send, final_recv,
 ):
     docs_at = lax.axis_index("docs")
     rep_at = lax.axis_index("rep")
@@ -186,9 +188,32 @@
     others = reps - 1
     candidates = fanout * per_owner
     score_scale = 2.0 / math.sqrt(width)
+    pull_scale = LOSS_SCALE * score_scale
+    block = width // reps
+    all_rows = reps * rows
+
+    loads = [
+        pltpu.make_async_copy(source, landing, load_sem.at[at])
+        for at, (source, landing) in enumerate(
+            (
+                (doc_hbm, doc_ref),
+                (queries_ref, raw_all.at[rep_at]),
+                (adapter_hbm, adapter_ref),
+                (routes_hbm, routes_all.at[rep_at]),
+                (doc_rows_hbm, meta_all.at[rep_at, pl.ds(0, candidates)]),
+                (labels_hbm, meta_all.at[rep_at, pl.ds(candidates, candidates)]),
+            )
+        )
+    ]
+    for load in loads:
+        load.start()
 
     def rep_peer(step):
         return lax.rem(rep_at + step, reps)
+
+    pair = rep_at + 1 - 2 * lax.rem(rep_at, 2)
+    cross = rep_peer(2)
+    pair_cross = lax.rem(pair + 2, reps)
 
     along, column = docs_at // 2, docs_at % 2
     place = along + column * (groups - 1 - 2 * along)
@@ -204,6 +229,7 @@
         pl.semaphore_signal(
             barrier, inc=1, device_id=(lax.rem(docs_at + step, groups), rep_at), device_id_type=MESH
         )
+    loads[0].wait()
     docs_all[0] = unit_rows(doc_ref[...])
     pl.semaphore_wait(barrier, others + groups - 1)
 
@@ -229,33 +255,40 @@
         for way in range(2):
             ring_copy(way, index).start()
 
-    def rep_copy(kind, at, source, landing):
-        return pltpu.make_async_remote_copy(
-            src_ref=source,
-            dst_ref=landing,
-            send_sem=rep_send.at[kind, at],
-            recv_sem=rep_recv.at[kind, at],
-            device_id=(docs_at, rep_peer(at + 1)),
-            device_id_type=MESH,
-        )
-
-    meta_copies = [rep_copy(0, at, meta_ref, meta_all.at[at]) for at in range(others)]
+    def rep_copies(kind, source, landing):
+        return [
+            pltpu.make_async_remote_copy(
+                src_ref=source(rep_peer(at + 1)),
+                dst_ref=landing(at),
+                send_sem=rep_send.at[kind, at],
+                recv_sem=rep_recv.at[kind, at],
+                device_id=(docs_at, rep_peer(at + 1)),
+                device_id_type=MESH,
+            )
+            for at in range(others)
+        ]
+
+    def own_block(ref):
+        return lambda at: ref.at[rep_at]
+
+    for load in loads[3:]:
+        load.wait()
+    meta_copies = rep_copies(0, own_block(meta_all), own_block(meta_all)) + rep_copies(
+        7, own_block(routes_all), own_block(routes_all)
+    )
     for copy in meta_copies:
         copy.start()
-    adapted = jnp.dot(queries_ref[...], adapter_ref[...], preferred_element_type=jnp.float32)
+    loads[1].wait()
+    loads[2].wait()
+    adapted = jnp.dot(raw_all[rep_at], adapter_ref[...], preferred_element_type=jnp.float32)
     radius = jnp.sqrt(jnp.mean(adapted * adapted, axis=-1, keepdims=True) + EPSILON)
-    unit_exact = adapted / radius
-    unit_exact_ref[...] = unit_exact
-    radius_ref[...] = radius
-    unit_all[others] = unit_exact.astype(jnp.bfloat16)
-    unit_copies = [rep_copy(1, at, unit_all.at[others], unit_all.at[at]) for at in range(others)]
-    for copy in unit_copies:
+    unit_all[rep_at] = (adapted / radius).astype(jnp.bfloat16)
+    radius_all[rep_at] = jnp.broadcast_to(radius, (rows, 128))
+    unit_copies = rep_copies(1, own_block(unit_all), own_block(unit_all))
+    radius_copies = rep_copies(2, own_block(radius_all), own_block(radius_all))
+    raw_copies = rep_copies(3, own_block(raw_all), own_block(raw_all))
+    for copy in unit_copies + radius_copies + raw_copies:
         copy.start()
-    raw_copies = [rep_copy(2, at, queries_ref, raw_all.at[at]) for at in range(others)]
-    for copy in raw_copies:
-        copy.start()
-    raw_all[others] = queries_ref[...]
-    meta_all[others] = meta_ref[...]
     stats[...] = jnp.zeros_like(stats)
 
     tile = 64
@@ -268,7 +301,7 @@
             at = index // tiles
             first = pl.multiple_of((index % tiles) * tile, tile)
             lanes = pl.ds(pl.multiple_of(at * rows, rows), rows)
-            owners = meta_all[at, 2 * candidates : 2 * candidates + 8, :]
+            owners = routes_all[at]
             ids = jnp.full((per_owner, rows), -1, jnp.int32)
             marks = jnp.zeros((per_owner, rows), jnp.int32)
             for k in range(fanout):
@@ -281,27 +314,27 @@
             found = jnp.zeros((tile, rows), jnp.float32)
             for m in range(per_owner):
                 found = jnp.where(here == ids[m : m + 1, :], marks[m : m + 1, :], found)
-            target_all[slot, pl.ds(first, tile), lanes] = found
+            marks_all[slot, pl.ds(first, tile), lanes] = found
             return carry
 
         lax.fori_loop(0, reps * tiles, step, 0)
 
     def score(slot):
         score_ref[...] = (
-            dot_nt(docs_all[slot], unit_all[...].reshape(reps * rows, width)) * score_scale
+            dot_nt(docs_all[slot], unit_all[...].reshape(all_rows, width)) * score_scale
         )
         for at in range(reps):
             lanes = pl.ds(at * rows, rows)
 
             def step(index, totals):
                 span = pl.ds(pl.multiple_of(index * tile, tile), tile)
-                marks = target_all[slot, span, lanes]
+                marks = marks_all[slot, span, lanes]
                 scores = score_ref[span, lanes]
                 held = marks > 0.5
                 raised = jnp.where(held, jnp.exp(scores), 0.0)
                 target = jnp.where(held, jnp.exp(marks - 1.0), 0.0) * label_sum[at, 0:1, :]
-                raised_all[slot, span, lanes] = raised
-                target_all[slot, span, lanes] = target * LOSS_SCALE
+                weight_ref[0, span, lanes] = raised.astype(jnp.bfloat16)
+                weight_ref[1, span, lanes] = (target * pull_scale).astype(jnp.bfloat16)
                 return (
                     totals[0] + jnp.sum(raised, axis=0, keepdims=True),
                     totals[1] + jnp.sum(target * scores, axis=0, keepdims=True),
@@ -311,6 +344,20 @@
             norm, dotted = lax.fori_loop(0, tiles, step, (zero, zero))
             stats[at, 0:1, :] += norm
             stats[at, 1:2, :] += dotted
+
+    def accumulate(slot, first):
+        for kind in range(2):
+            turned = weight_ref[kind].T
+            for at in range(reps):
+                term = jnp.dot(
+                    turned,
+                    docs_all[slot, :, at * block : (at + 1) * block],
+                    preferred_element_type=jnp.float32,
+                )
+                if first:
+                    sums[at, kind] = term
+                else:
+                    sums[at, kind] += term
 
     for index in range(ring_steps):
         for way in range(2):
@@ -333,130 +380,157 @@
         elif index == 2:
             for copy in unit_copies:
                 copy.wait_recv()
-            score(0)
-            score(1)
+            for slot in (0, 1):
+                score(slot)
+                accumulate(slot, slot == 0)
+        elif index == 3:
             score(groups - 1)
+            accumulate(groups - 1, False)
         elif index % 2 == 0:
-            score(index // 2)
-            score(groups - index // 2)
+            for slot in (index // 2, groups - index // 2):
+                score(slot)
+                accumulate(slot, False)
     score(groups // 2)
-
-    def small_copy(kind, at, peer, source, landing):
+    stat_copies = rep_copies(4, lambda at: stats, lambda at: stats_in.at[at])
+    for copy in stat_copies:
+        copy.start()
+    accumulate(groups // 2, False)
+
+    def pull_copy(at, source, landing, peer):
         return pltpu.make_async_remote_copy(
             src_ref=source,
             dst_ref=landing,
-            send_sem=small_send.at[kind, at],
-            recv_sem=small_recv.at[kind, at],
+            send_sem=pull_send.at[at],
+            recv_sem=pull_recv.at[at],
             device_id=(docs_at, peer),
             device_id_type=MESH,
         )
 
-    stat_copies = [
-        small_copy(0, at, rep_peer(at + 1), stats, stats_in.at[at]) for at in range(others)
-    ]
-    for copy in stat_copies:
-        copy.start()
+    pair_out[...] = sums[pair_cross].astype(jnp.bfloat16)
+    pair_copy = pull_copy(0, pair_out, pair_in, pair)
+    pair_copy.start()
     for copy in stat_copies:
         copy.wait_recv()
-    norms = []
+    shares = []
     for at in range(reps):
         total = stats[at]
         for origin in range(others):
-            total = total + stats_in[origin, (at - origin - 1) % reps]
-        norms.append(total)
-    loss_ref[...] = jnp.log(norms[others][0:1, :]) - norms[others][1:2, :]
-
-    pull_copies = [
-        small_copy(1, at, rep_peer(reps - at - 1), pull_out.at[at], pull_in.at[at])
-        for at in range(others)
-    ]
-    all_docs = docs_all[...].reshape(groups * doc_count, width)
-    own_pull = None
-    for pair in range(reps // 2):
-        for at in (2 * pair, 2 * pair + 1):
-            share = LOSS_SCALE / norms[at][0:1, :]
-            lanes = pl.ds(at * rows, rows)
-
-            def weigh(slot, carry):
-                weight_ref[slot, :, lanes] = (
-                    raised_all[slot, :, lanes] * share - target_all[slot, :, lanes]
-                ).astype(jnp.bfloat16)
-                return carry
-
-            lax.fori_loop(0, groups, weigh, 0)
-        lanes = pl.ds(2 * pair * rows, 2 * rows)
-        pulled = (
-            dot_tn(weight_ref[:, :, lanes].reshape(groups * doc_count, 2 * rows), all_docs)
-            * score_scale
-        )
-        for at in (2 * pair, 2 * pair + 1):
-            low = (at - 2 * pair) * rows
-            if at < others:
-                pull_out[at] = pulled[low : low + rows].astype(jnp.bfloat16)
-                pull_copies[at].start()
-            else:
-                own_pull = pulled[low : low + rows]
-    pull_total = own_pull
-    for at in range(others):
-        pull_copies[at].wait_recv()
-        pull_total = pull_total + pull_in[at].astype(jnp.float32)
-    unit = unit_exact_ref[...]
-    projection = jnp.mean(unit * pull_total, axis=-1, keepdims=True)
-    adapted_grad = ((pull_total - unit * projection) / radius_ref[...]).astype(jnp.bfloat16)
-    block = width // reps
+            total = total + stats_in[origin, at]
+        stats_in[0, at] = total
+        shares.append((pull_scale / total).T[:, 0:1])
+    own_stats = stats_in[0, rep_at]
+    loss_ref[...] = jnp.log(own_stats[0:1, :]) - own_stats[1:2, :]
+    pair_copy.wait_recv()
+    cross_copies = []
     for at in range(reps):
-        grad_cols[at] = adapted_grad[:, at * block : (at + 1) * block]
-    grad_copies = [
-        small_copy(2, at, rep_peer(at + 1), grad_cols.at[rep_peer(at + 1)], grad_in.at[at])
-        for at in range(others)
-    ]
+        span = pl.ds(at * rows, rows)
+        raised = sums[cross, 0, span, :] + pair_in[0, span, :].astype(jnp.float32)
+        target = sums[cross, 1, span, :] + pair_in[1, span, :].astype(jnp.float32)
+        cross_out[at] = (raised * shares[at] - target).astype(jnp.bfloat16)
+        copy = pull_copy(2 + at, cross_out.at[at], cross_in.at[at], cross)
+        copy.start()
+        cross_copies.append(copy)
+    for at in range(reps):
+        span = pl.ds(at * rows, rows)
+        near_out[at] = (sums[pair, 0, span, :] * shares[at] - sums[pair, 1, span, :]).astype(
+            jnp.bfloat16
+        )
+    near_copy = pull_copy(1, near_out, near_in, pair)
+    near_copy.start()
+    for at in range(reps):
+        span = pl.ds(at * rows, rows)
+        pull_ref[at] = sums[rep_at, 0, span, :] * shares[at] - sums[rep_at, 1, span, :]
+    near_copy.wait_recv()
+    ones = jnp.ones((8, block), jnp.bfloat16)
+    own_cols = pl.ds(pl.multiple_of(rep_at * block, block), block)
+    for at in range(reps):
+        held = pull_ref[at] + near_in[at].astype(jnp.float32)
+        cross_copies[at].wait_recv()
+        held = held + cross_in[at].astype(jnp.float32)
+        pull_ref[at] = held
+        unit = unit_all[at, :, own_cols].astype(jnp.float32)
+        project_out[at] = dot_nt(ones, (unit * held).astype(jnp.bfloat16))
+    project_copies = rep_copies(5, lambda at: project_out, lambda at: project_in.at[at])
+    for copy in project_copies:
+        copy.start()
+    for copy in radius_copies + raw_copies + project_copies:
+        copy.wait_recv()
+    for at in range(reps):
+        total = project_out[at]
+        for origin in range(others):
+            total = total + project_in[origin, at]
+        projection = (total * (1.0 / width)).T[:, 0:1]
+        unit = unit_all[at, :, own_cols].astype(jnp.float32)
+        grad_cols[at] = ((pull_ref[at] - unit * projection) / radius_all[at, :, 0:1]).astype(
+            jnp.bfloat16
+        )
+    grad_copies = rep_copies(6, lambda peer: grad_cols.at[peer], own_block(grad_home))
     for copy in grad_copies:
         copy.start()
-    grad_in[others] = grad_cols[rep_at]
-    query_grad_ref[...] = dot_nt(adapted_grad, adapter_ref[...]).astype(jnp.bfloat16)
-    for at in range(others):
-        raw_copies[at].wait_recv()
-        grad_copies[at].wait_recv()
+    grad_home[rep_at] = grad_cols[rep_at]
+
+    out_rows = width // groups
+    parts = 2
+    piece = block // parts
     group_terms = dot_tn(
-        raw_all[...].reshape(reps * rows, width), grad_in[...].reshape(reps * rows, block)
-    )
-    out_rows = width // groups
-    terms_out[...] = group_terms.astype(jnp.bfloat16).reshape(groups, out_rows, block)
+        raw_all[...].reshape(all_rows, width), grad_cols[...].reshape(all_rows, block)
+    ).astype(jnp.bfloat16).reshape(groups, out_rows, block)
+    for part in range(parts):
+        terms_out[part] = group_terms[:, :, part * piece : (part + 1) * piece]
+    far_first = sorted(range(1, groups), key=lambda step: abs(step - groups // 2))
     term_copies = []
-    for step in range(1, groups):
-        peer = lax.rem(docs_at + step, groups)
-        copy = pltpu.make_async_remote_copy(
-            src_ref=terms_out.at[peer],
-            dst_ref=terms_in.at[step - 1],
-            send_sem=terms_send.at[step - 1],
-            recv_sem=terms_recv.at[step - 1],
-            device_id=(peer, rep_at),
-            device_id_type=MESH,
-        )
-        copy.start()
-        term_copies.append(copy)
-    summed = terms_out[docs_at].astype(jnp.float32)
-    for step in range(groups - 1):
-        term_copies[step].wait_recv()
-        summed = summed + terms_in[step].astype(jnp.float32)
-    final_cols[rep_at] = (summed * inverse_root).astype(jnp.bfloat16)
-    final_copies = [
-        small_copy(3, at, rep_peer(at + 1), final_cols.at[rep_at], final_cols.at[rep_at])
-        for at in range(others)
-    ]
-    for copy in final_copies:
-        copy.start()
-    for copy in final_copies:
+    for part in range(parts):
+        for step in far_first:
+            peer = lax.rem(docs_at + step, groups)
+            copy = pltpu.make_async_remote_copy(
+                src_ref=terms_out.at[part, peer],
+                dst_ref=terms_in.at[part, step - 1],
+                send_sem=terms_send.at[part, step - 1],
+                recv_sem=terms_recv.at[part, step - 1],
+                device_id=(peer, rep_at),
+                device_id_type=MESH,
+            )
+            copy.start()
+            term_copies.append(copy)
+    for copy in grad_copies:
         copy.wait_recv()
-    for at in range(reps):
-        adapter_grad_ref[:, at * block : (at + 1) * block] = final_cols[at]
+    query_grad = dot_nt(grad_home[0], adapter_ref[:, 0:block])
+    for at in range(1, reps):
+        query_grad += dot_nt(grad_home[at], adapter_ref[:, at * block : (at + 1) * block])
+    query_grad_ref[...] = query_grad.astype(jnp.bfloat16)
+    final_copies = []
+    for part in range(parts):
+        summed = terms_out[part, docs_at].astype(jnp.float32)
+        for at in range(groups - 1):
+            term_copies[part * (groups - 1) + at].wait_recv()
+        for at in range(groups - 1):
+            summed = summed + terms_in[part, at].astype(jnp.float32)
+        final_cols[part, rep_at] = (summed * inverse_root).astype(jnp.bfloat16)
+        for at in range(others):
+            copy = pltpu.make_async_remote_copy(
+                src_ref=final_cols.at[part, rep_at],
+                dst_ref=final_cols.at[part, rep_at],
+                send_sem=final_send.at[part, at],
+                recv_sem=final_recv.at[part, at],
+                device_id=(docs_at, rep_peer(at + 1)),
+                device_id_type=MESH,
+            )
+            copy.start()
+            final_copies.append(copy)
+    for part in range(parts):
+        for at in range(others):
+            final_copies[part * others + at].wait_recv()
+        for at in range(reps):
+            low = at * block + part * piece
+            adapter_grad_ref[:, low : low + piece] = final_cols[part, at]
 
     for index in range(ring_steps):
         for way in range(2):
             ring_copy(way, index).wait_send()
     for copy in (
-        meta_copies + unit_copies + raw_copies + stat_copies + pull_copies
-        + grad_copies + term_copies + final_copies
+        meta_copies + unit_copies + radius_copies + raw_copies + stat_copies
+        + [pair_copy, near_copy] + cross_copies + project_copies + grad_copies
+        + term_copies + final_copies
     ):
         copy.wait_send()
 
@@ -472,16 +546,7 @@
     block = width // reps
     out_rows = width // groups
     others = reps - 1
-    meta = jnp.concatenate(
-        [
-            doc_rows.reshape(rows, candidates),
-            labels.reshape(rows, candidates),
-            routes,
-            jnp.zeros((rows, 8 - fanout), jnp.int32),
-        ],
-        axis=1,
-    ).T
-    meta_rows = meta.shape[0]
+    all_rows = reps * rows
     bf16, f32 = jnp.bfloat16, jnp.float32
     vmem = pltpu.VMEM
     dma = pltpu.SemaphoreType.DMA
@@ -495,48 +560,63 @@
             jax.ShapeDtypeStruct((rows, width), bf16),
             jax.ShapeDtypeStruct((out_rows, width), bf16),
         ),
-        in_specs=[pl.BlockSpec(memory_space=vmem)] * 4,
+        in_specs=[pl.BlockSpec(memory_space=pl.ANY)] * 6,
         out_specs=[pl.BlockSpec(memory_space=vmem)] * 3,
         scratch_shapes=[
+            vmem((width, width), bf16),
+            vmem((doc_count, width), bf16),
             vmem((groups, doc_count, width), bf16),
             vmem((reps, rows, width), bf16),
             vmem((reps, rows, width), bf16),
-            vmem((reps, meta_rows, rows), jnp.int32),
-            vmem((rows, width), f32),
-            vmem((rows, 1), f32),
-            vmem((groups, doc_count, reps * rows), f32),
-            vmem((groups, doc_count, reps * rows), f32),
-            vmem((doc_count, reps * rows), f32),
+            vmem((reps, 2 * candidates, rows), jnp.int32),
+            vmem((reps, fanout, rows), jnp.int32),
+            vmem((reps, rows, 128), f32),
+            vmem((groups, doc_count, all_rows), f32),
+            vmem((doc_count, all_rows), f32),
+            vmem((2, doc_count, all_rows), bf16),
+            vmem((reps, 2, all_rows, block), f32),
             vmem((reps, 8, rows), f32),
             vmem((reps, 8, rows), f32),
             vmem((others, reps, 8, rows), f32),
-            vmem((groups, doc_count, reps * rows), bf16),
-            vmem((others, rows, width), bf16),
-            vmem((others, rows, width), bf16),
+            vmem((2, all_rows, block), bf16),
+            vmem((2, all_rows, block), bf16),
             vmem((reps, rows, block), bf16),
             vmem((reps, rows, block), bf16),
-            vmem((groups, out_rows, block), bf16),
-            vmem((groups - 1, out_rows, block), bf16),
-            vmem((reps, out_rows, block), bf16),
+            vmem((reps, rows, block), bf16),
+            vmem((reps, rows, block), bf16),
+            vmem((reps, rows, block), f32),
+            vmem((reps, 8, rows), f32),
+            vmem((others, reps, 8, rows), f32),
+            vmem((reps, rows, block), bf16),
+            vmem((reps, rows, block), bf16),
+            vmem((2, groups, out_rows, block // 2), bf16),
+            vmem((2, groups - 1, out_rows, block // 2), bf16),
+            vmem((2, reps, out_rows, block // 2), bf16),
+            dma((6,)),
             dma((2, groups - 1)),
             dma((2, groups - 1)),
-            dma((3, others)),
-            dma((3, others)),
-            dma((4, others)),
-            dma((4, others)),
-            dma((groups - 1,)),
-            dma((groups - 1,)),
+            dma((8, others)),
+            dma((8, others)),
+            dma((2 + reps,)),
+            dma((2 + reps,)),
+            dma((2, groups - 1)),
+            dma((2, groups - 1)),
+            dma((2, others)),
+            dma((2, others)),
         ],
         compiler_params=pltpu.CompilerParams(
-            collective_id=0, has_side_effects=True, vmem_limit_bytes=48 * 1024 * 1024
+            collective_id=0, has_side_effects=True, vmem_limit_bytes=56 * 1024 * 1024
         ),
-    )(queries, adapter, doc_table, meta)
+    )(
+        queries, adapter, doc_table, routes.T,
+        doc_rows.reshape(rows, candidates).T, labels.reshape(rows, candidates).T,
+    )
     return (losses.reshape(rows), query_grads, adapter_grad)
 
 
 def on_device(queries, adapter, doc_table, routes, doc_rows, labels):
     gathered_bytes = lax.axis_size("docs") * doc_table.size * doc_table.dtype.itemsize
-    if gathered_bytes <= GATHER_LIMIT and lax.axis_size("rep") % 2 == 0:
+    if gathered_bytes <= GATHER_LIMIT and lax.axis_size("rep") == 4:
         return gathered_on_device(queries, adapter, doc_table, routes, doc_rows, labels)
     return routed_on_device(queries, adapter, doc_table, routes, doc_rows, labels)
 

time: 96.4 us -> 88 us (0.913)
  the two profiles are of different devices: /device:TPU:15 before, /device:TPU:0 now
where the time goes in v2:
time: 88 us; the launch traced here: 87.8 us
  Pallas kernels  82.8 us (94%)
  local copies, waits for them, and re-layouts  4.44 us (5%)
    pallas_call x1, Pallas kernels, gathered_on_device(): pl.pallas_call(functools.partial(gathered_kernel, groups, reps, fanout, p...  82.8 us
    unnamed x3, local copies, waits for them, and re-layouts  4.44 us

profile of v2, /device:TPU:0, one launch (start us, length us, event | category | flops | bytes accessed | tf_op | source)
XLA Modules:
  0.0 87.8 jit_solution(4728010491712575056)
XLA Ops:
  0.6 82.8 %shard_map.85 = (f32[1,128]{1,0:T(1,128)}, bf16[128,1024]{1,0:T(8,128)(2,1)}, bf16[128,1024]{1,0:T(8,128)(2,1)}) custom-call(bf16[128,1024]{1,0:T(8,128)(2,1)} %queries_ref.1, bf16[1024,1024]{1,0:T(8,128)(2,1)} %adapter_hbm.1, bf16[256,1024]{1,0:T(8,128)(2,1)} %doc_hbm.1, s32[4,128]{1,0:T(4,128)} %bitcast.10, s32[64,128]{1,0:T(8,128)} %bitcast.8, ...), custom_call_target="tpu_custom_call" | custom-call | tf_op jit(solution)/shard_map/pallas_call | solution.py:553
  83.4 1.1 %copy.12 = f32[128]{0:T(128)} copy(f32[128]{0:T(128)} %bitcast.11) | data formatting | bytes 1024
  84.5 1.7 %copy.13 = bf16[128,1024]{1,0:T(8,128)(2,1)} copy(bf16[128,1024]{1,0:T(8,128)(2,1)} %get-tuple-element.13) | data formatting | bytes 524288
  86.2 1.7 %copy.14 = bf16[128,1024]{1,0:T(8,128)(2,1)} copy(bf16[128,1024]{1,0:T(8,128)(2,1)} %get-tuple-element.14) | data formatting | bytes 524288

commit v3 on v2

--- a/solution.py
+++ b/solution.py
@@ -158,10 +158,6 @@
     return lax.dot_general(a, b, (((1,), (1,)), ((), ())), preferred_element_type=jnp.float32)
 
 
-def dot_tn(a, b):
-    return lax.dot_general(a, b, (((0,), (0,)), ((), ())), preferred_element_type=jnp.float32)
-
-
 def ring_group(position, groups):
     column = position // (groups // 2)
     along = position + column * (groups - 1 - 2 * position)
@@ -170,10 +166,10 @@
 
 def gathered_kernel(
     groups, reps, fanout, per_owner, inverse_root,
-    queries_ref, adapter_hbm, doc_hbm, routes_hbm, doc_rows_hbm, labels_hbm,
+    queries_ref, adapter_hbm, doc_hbm, meta_hbm,
     loss_ref, query_grad_ref, adapter_grad_ref,
-    adapter_ref, doc_ref, docs_all, unit_all, raw_all, meta_all, routes_all, radius_all,
-    marks_all, score_ref, weight_ref, sums, label_sum, stats, stats_in,
+    adapter_ref, doc_ref, docs_all, unit_all, raw_all, meta_all, radius_all,
+    marks_all, here_ref, raw_turned, score_ref, weight_ref, sums, label_sum, stats, stats_in,
     pair_out, pair_in, cross_out, cross_in, near_out, near_in, pull_ref,
     project_out, project_in, grad_cols, grad_home,
     terms_out, terms_in, final_cols,
@@ -199,9 +195,7 @@
                 (doc_hbm, doc_ref),
                 (queries_ref, raw_all.at[rep_at]),
                 (adapter_hbm, adapter_ref),
-                (routes_hbm, routes_all.at[rep_at]),
-                (doc_rows_hbm, meta_all.at[rep_at, pl.ds(0, candidates)]),
-                (labels_hbm, meta_all.at[rep_at, pl.ds(candidates, candidates)]),
+                (meta_hbm, meta_all.at[rep_at]),
             )
         )
     ]
@@ -271,11 +265,8 @@
     def own_block(ref):
         return lambda at: ref.at[rep_at]
 
-    for load in loads[3:]:
-        load.wait()
-    meta_copies = rep_copies(0, own_block(meta_all), own_block(meta_all)) + rep_copies(
-        7, own_block(routes_all), own_block(routes_all)
-    )
+    loads[3].wait()
+    meta_copies = rep_copies(0, own_block(meta_all), own_block(meta_all))
     for copy in meta_copies:
         copy.start()
     loads[1].wait()
@@ -287,9 +278,12 @@
     unit_copies = rep_copies(1, own_block(unit_all), own_block(unit_all))
     radius_copies = rep_copies(2, own_block(radius_all), own_block(radius_all))
     raw_copies = rep_copies(3, own_block(raw_all), own_block(raw_all))
-    for copy in unit_copies + radius_copies + raw_copies:
+    for copy in unit_copies + radius_copies:
         copy.start()
     stats[...] = jnp.zeros_like(stats)
+    here_ref[...] = (
+        lax.broadcasted_iota(jnp.int32, (doc_count, rows), 0).astype(jnp.float32).astype(jnp.bfloat16)
+    )
 
     tile = 64
     tiles = doc_count // tile
@@ -301,7 +295,7 @@
             at = index // tiles
             first = pl.multiple_of((index % tiles) * tile, tile)
             lanes = pl.ds(pl.multiple_of(at * rows, rows), rows)
-            owners = routes_all[at]
+            owners = meta_all[at, 2 * candidates : 2 * candidates + 8, :]
             ids = jnp.full((per_owner, rows), -1, jnp.int32)
             marks = jnp.zeros((per_owner, rows), jnp.int32)
             for k in range(fanout):
@@ -309,9 +303,10 @@
                 ids = jnp.where(named, meta_all[at, k * per_owner : (k + 1) * per_owner, :], ids)
                 low = candidates + k * per_owner
                 marks = jnp.where(named, meta_all[at, low : low + per_owner, :] + 1, marks)
-            marks = marks.astype(jnp.float32)
-            here = lax.broadcasted_iota(jnp.int32, (tile, rows), 0) + first
-            found = jnp.zeros((tile, rows), jnp.float32)
+            ids = ids.astype(jnp.float32).astype(jnp.bfloat16)
+            marks = marks.astype(jnp.float32).astype(jnp.bfloat16)
+            here = here_ref[pl.ds(first, tile), :]
+            found = jnp.zeros((tile, rows), jnp.bfloat16)
             for m in range(per_owner):
                 found = jnp.where(here == ids[m : m + 1, :], marks[m : m + 1, :], found)
             marks_all[slot, pl.ds(first, tile), lanes] = found
@@ -319,7 +314,7 @@
 
         lax.fori_loop(0, reps * tiles, step, 0)
 
-    def score(slot):
+    def score(slot, buffer):
         score_ref[...] = (
             dot_nt(docs_all[slot], unit_all[...].reshape(all_rows, width)) * score_scale
         )
@@ -328,13 +323,13 @@
 
             def step(index, totals):
                 span = pl.ds(pl.multiple_of(index * tile, tile), tile)
-                marks = marks_all[slot, span, lanes]
+                marks = marks_all[slot, span, lanes].astype(jnp.float32)
                 scores = score_ref[span, lanes]
                 held = marks > 0.5
                 raised = jnp.where(held, jnp.exp(scores), 0.0)
                 target = jnp.where(held, jnp.exp(marks - 1.0), 0.0) * label_sum[at, 0:1, :]
-                weight_ref[0, span, lanes] = raised.astype(jnp.bfloat16)
-                weight_ref[1, span, lanes] = (target * pull_scale).astype(jnp.bfloat16)
+                weight_ref[buffer, 0, span, lanes] = raised.astype(jnp.bfloat16)
+                weight_ref[buffer, 1, span, lanes] = (target * pull_scale).astype(jnp.bfloat16)
                 return (
                     totals[0] + jnp.sum(raised, axis=0, keepdims=True),
                     totals[1] + jnp.sum(target * scores, axis=0, keepdims=True),
@@ -345,26 +340,25 @@
             stats[at, 0:1, :] += norm
             stats[at, 1:2, :] += dotted
 
-    def accumulate(slot, first):
+    def accumulate(slots, first):
         for kind in range(2):
-            turned = weight_ref[kind].T
+            turned = [weight_ref[buffer, kind].T for buffer in range(len(slots))]
             for at in range(reps):
-                term = jnp.dot(
-                    turned,
-                    docs_all[slot, :, at * block : (at + 1) * block],
-                    preferred_element_type=jnp.float32,
-                )
+                terms = [
+                    jnp.dot(
+                        part,
+                        docs_all[slot, :, at * block : (at + 1) * block],
+                        preferred_element_type=jnp.float32,
+                    )
+                    for part, slot in zip(turned, slots)
+                ]
                 if first:
-                    sums[at, kind] = term
+                    sums[at, kind] = sum(terms)
                 else:
-                    sums[at, kind] += term
-
-    for index in range(ring_steps):
-        for way in range(2):
-            ring_copy(way, index).wait_recv()
-            if index + 2 < ring_steps:
-                ring_copy(way, index + 2).start()
-        if index == 0:
+                    sums[at, kind] += sum(terms)
+
+    def between(index, way):
+        if index == 0 and way == 0:
             for copy in meta_copies:
                 copy.wait_recv()
             for at in range(reps):
@@ -372,29 +366,49 @@
                     meta_all[at, candidates : 2 * candidates, :].astype(jnp.float32)
                 )
                 label_sum[at, 0:1, :] = 1.0 / jnp.sum(raised_labels, axis=0, keepdims=True)
-            for slot in range(4):
+        if index < 2:
+            share = groups // 4
+            first = (2 * index + way) * share
+            for slot in range(first, first + share):
                 label_mask(slot)
-        elif index == 1:
-            for slot in range(4, groups):
-                label_mask(slot)
-        elif index == 2:
+        elif index == 2 and way == 0:
             for copy in unit_copies:
                 copy.wait_recv()
-            for slot in (0, 1):
-                score(slot)
-                accumulate(slot, slot == 0)
-        elif index == 3:
-            score(groups - 1)
-            accumulate(groups - 1, False)
-        elif index % 2 == 0:
-            for slot in (index // 2, groups - index // 2):
-                score(slot)
-                accumulate(slot, False)
-    score(groups // 2)
+            for copy in raw_copies:
+                copy.start()
+            score(0, 0)
+            accumulate((0,), True)
+        elif index == 2:
+            score(1, 0)
+        elif index == 3 and way == 0:
+            score(groups - 1, 1)
+            accumulate((1, groups - 1), False)
+        elif index % 2 == 0 and way == 0 and index < ring_steps - 1:
+            score(index // 2, 0)
+        elif index % 2 == 0 and index < ring_steps - 1:
+            score(groups - index // 2, 1)
+            accumulate((index // 2, groups - index // 2), False)
+        elif index == ring_steps - 2 and way == 0:
+            score(groups // 2 - 1, 0)
+        elif index == ring_steps - 2:
+            score(groups // 2 + 1, 1)
+            accumulate((groups // 2 - 1, groups // 2 + 1), False)
+            for copy in raw_copies:
+                copy.wait_recv()
+            for at in range(reps):
+                raw_turned[:, at * rows : (at + 1) * rows] = raw_all[at].T
+
+    for index in range(ring_steps):
+        for way in range(2):
+            ring_copy(way, index).wait_recv()
+            if index + 2 < ring_steps:
+                ring_copy(way, index + 2).start()
+            between(index, way)
+    score(groups // 2, 0)
     stat_copies = rep_copies(4, lambda at: stats, lambda at: stats_in.at[at])
     for copy in stat_copies:
         copy.start()
-    accumulate(groups // 2, False)
+    accumulate((groups // 2,), False)
 
     def pull_copy(at, source, landing, peer):
         return pltpu.make_async_remote_copy(
@@ -453,7 +467,7 @@
     project_copies = rep_copies(5, lambda at: project_out, lambda at: project_in.at[at])
     for copy in project_copies:
         copy.start()
-    for copy in radius_copies + raw_copies + project_copies:
+    for copy in radius_copies + project_copies:
         copy.wait_recv()
     for at in range(reps):
         total = project_out[at]
@@ -472,8 +486,8 @@
     out_rows = width // groups
     parts = 2
     piece = block // parts
-    group_terms = dot_tn(
-        raw_all[...].reshape(all_rows, width), grad_cols[...].reshape(all_rows, block)
+    group_terms = jnp.dot(
+        raw_turned[...], grad_cols[...].reshape(all_rows, block), preferred_element_type=jnp.float32
     ).astype(jnp.bfloat16).reshape(groups, out_rows, block)
     for part in range(parts):
         terms_out[part] = group_terms[:, :, part * piece : (part + 1) * piece]
@@ -547,6 +561,15 @@
     out_rows = width // groups
     others = reps - 1
     all_rows = reps * rows
+    meta = jnp.concatenate(
+        [
+            doc_rows.reshape(rows, candidates),
+            labels.reshape(rows, candidates),
+            routes,
+            jnp.zeros((rows, 8 - fanout), jnp.int32),
+        ],
+        axis=1,
+    ).T
     bf16, f32 = jnp.bfloat16, jnp.float32
     vmem = pltpu.VMEM
     dma = pltpu.SemaphoreType.DMA
@@ -560,7 +583,7 @@
             jax.ShapeDtypeStruct((rows, width), bf16),
             jax.ShapeDtypeStruct((out_rows, width), bf16),
         ),
-        in_specs=[pl.BlockSpec(memory_space=pl.ANY)] * 6,
+        in_specs=[pl.BlockSpec(memory_space=pl.ANY)] * 4,
         out_specs=[pl.BlockSpec(memory_space=vmem)] * 3,
         scratch_shapes=[
             vmem((width, width), bf16),
@@ -568,12 +591,13 @@
             vmem((groups, doc_count, width), bf16),
             vmem((reps, rows, width), bf16),
             vmem((reps, rows, width), bf16),
-            vmem((reps, 2 * candidates, rows), jnp.int32),
-            vmem((reps, fanout, rows), jnp.int32),
+            vmem((reps, 2 * candidates + 8, rows), jnp.int32),
             vmem((reps, rows, 128), f32),
-            vmem((groups, doc_count, all_rows), f32),
+            vmem((groups, doc_count, all_rows), bf16),
+            vmem((doc_count, rows), bf16),
+            vmem((width, all_rows), bf16),
             vmem((doc_count, all_rows), f32),
-            vmem((2, doc_count, all_rows), bf16),
+            vmem((2, 2, doc_count, all_rows), bf16),
             vmem((reps, 2, all_rows, block), f32),
             vmem((reps, 8, rows), f32),
             vmem((reps, 8, rows), f32),
@@ -592,11 +616,11 @@
             vmem((2, groups, out_rows, block // 2), bf16),
             vmem((2, groups - 1, out_rows, block // 2), bf16),
             vmem((2, reps, out_rows, block // 2), bf16),
-            dma((6,)),
+            dma((4,)),
             dma((2, groups - 1)),
             dma((2, groups - 1)),
-            dma((8, others)),
-            dma((8, others)),
+            dma((7, others)),
+            dma((7, others)),
             dma((2 + reps,)),
             dma((2 + reps,)),
             dma((2, groups - 1)),
@@ -605,11 +629,10 @@
             dma((2, others)),
         ],
         compiler_params=pltpu.CompilerParams(
-            collective_id=0, has_side_effects=True, vmem_limit_bytes=56 * 1024 * 1024
+            collective_id=0, has_side_effects=True, vmem_limit_bytes=213 * 256 * 1024
         ),
     )(
-        queries, adapter, doc_table, routes.T,
-        doc_rows.reshape(rows, candidates).T, labels.reshape(rows, candidates).T,
+        queries, adapter, doc_table, meta,
     )
     return (losses.reshape(rows), query_grads, adapter_grad)
 

time: 88 us -> 82.7 us (0.940)
  Pallas kernels: 82.8 us -> 79 us
  local copies, waits for them, and re-layouts: 4.44 us -> 1.99 us
    pallas_call x1, Pallas kernels: 82.8 us -> 79 us  [gathered_on_device(): pl.pallas_call(functools.partial(gathered_kernel, groups, reps, fanout, p...]
    unnamed x3, local copies, waits for them, and re-layouts: 4.44 us -> 1.92 us
where the time goes in v3:
time: 82.7 us; the launch traced here: 82.5 us
  Pallas kernels  79 us (96%)
  local copies, waits for them, and re-layouts  1.99 us (2%)
  other arithmetic  0.87 us (1%)
    pallas_call x1, Pallas kernels, gathered_on_device(): pl.pallas_call(functools.partial(gathered_kernel, groups, reps, fanout, p...  79 us
    unnamed x3, local copies, waits for them, and re-layouts  1.92 us

profile of v3, /device:TPU:0, one launch (start us, length us, event | category | flops | bytes accessed | tf_op | source)
XLA Modules:
  0.0 82.5 jit_solution(2885685536877761316)
XLA Ops:
  0.6 0.1 pad.3.clone
  0.7 0.9 %add_bitcast_fusion.meta_hbm = s32[136,128]{1,0:T(8,128)S(1)} fusion(s32[128,4]{0,1:T(4,128)} %param.9, s32[128,64]{0,1:T(8,128)} %bitcast.6, s32[128,64]{0,1:T(8,128)} %bitcast.7, s32[136]{0:T(256)S(1)} %pad.3.clone), kind=kLoop, calls=%fused_computation | loop fusion | flops 52224 | bytes 137760 | tf_op jit(solution)/shard_map/transpose | solution.py:572
  1.6 79.0 %shard_map.85 = (f32[1,128]{1,0:T(1,128)S(1)}, bf16[128,1024]{1,0:T(8,128)(2,1)S(1)}, bf16[128,1024]{1,0:T(8,128)(2,1)S(1)}) custom-call(bf16[128,1024]{1,0:T(8,128)(2,1)} %queries_ref.1, bf16[1024,1024]{1,0:T(8,128)(2,1)} %adapter_hbm.1, bf16[256,1024]{1,0:T(8,128)(2,1)} %doc_hbm.1, s32[136,128]{1,0:T(8,128)S(1)} %add_bitcast_fusion.meta_hbm), custom_call_target="tpu_custom_call" | custom-call | tf_op jit(solution)/shard_map/pallas_call | solution.py:576
  80.6 0.5 copy.12
  81.1 0.7 copy.13
  81.8 0.7 copy.14
  (1 shorter events, 0.0 us)

commit v4 on v3

--- a/solution.py
+++ b/solution.py
@@ -171,7 +171,7 @@
     adapter_ref, doc_ref, docs_all, unit_all, raw_all, meta_all, radius_all,
     marks_all, here_ref, raw_turned, score_ref, weight_ref, sums, label_sum, stats, stats_in,
     pair_out, pair_in, cross_out, cross_in, near_out, near_in, pull_ref,
-    project_out, project_in, grad_cols, grad_home,
+    grad_cols, grad_home,
     terms_out, terms_in, final_cols,
     load_sem, ring_send, ring_recv, rep_send, rep_recv, pull_send, pull_recv,
     terms_send, terms_recv, final_send, final_recv,
@@ -278,7 +278,7 @@
     unit_copies = rep_copies(1, own_block(unit_all), own_block(unit_all))
     radius_copies = rep_copies(2, own_block(radius_all), own_block(radius_all))
     raw_copies = rep_copies(3, own_block(raw_all), own_block(raw_all))
-    for copy in unit_copies + radius_copies:
+    for copy in unit_copies:
         copy.start()
     stats[...] = jnp.zeros_like(stats)
     here_ref[...] = (
@@ -289,22 +289,29 @@
     tiles = doc_count // tile
 
     def label_mask(slot):
-        owner = ring_group(lax.rem(place + groups - slot, groups), groups) * reps + rep_at
+        owner = (
+            ring_group(lax.rem(place + groups - slot, groups), groups) * reps + rep_at
+        ).astype(jnp.float32)
 
         def step(index, carry):
             at = index // tiles
             first = pl.multiple_of((index % tiles) * tile, tile)
             lanes = pl.ds(pl.multiple_of(at * rows, rows), rows)
-            owners = meta_all[at, 2 * candidates : 2 * candidates + 8, :]
-            ids = jnp.full((per_owner, rows), -1, jnp.int32)
-            marks = jnp.zeros((per_owner, rows), jnp.int32)
+            owners = meta_all[at, 2 * candidates : 2 * candidates + 16, :].astype(jnp.float32)
+            ids = jnp.full((per_owner, rows), -1.0, jnp.float32)
+            marks = jnp.zeros((per_owner, rows), jnp.float32)
             for k in range(fanout):
                 named = owners[k : k + 1, :] == owner
-                ids = jnp.where(named, meta_all[at, k * per_owner : (k + 1) * per_owner, :], ids)
+                low = k * per_owner
+                ids = jnp.where(
+                    named, meta_all[at, low : low + per_owner, :].astype(jnp.float32), ids
+                )
                 low = candidates + k * per_owner
-                marks = jnp.where(named, meta_all[at, low : low + per_owner, :] + 1, marks)
-            ids = ids.astype(jnp.float32).astype(jnp.bfloat16)
-            marks = marks.astype(jnp.float32).astype(jnp.bfloat16)
+                marks = jnp.where(
+                    named, meta_all[at, low : low + per_owner, :].astype(jnp.float32) + 1.0, marks
+                )
+            ids = ids.astype(jnp.bfloat16)
+            marks = marks.astype(jnp.bfloat16)
             here = here_ref[pl.ds(first, tile), :]
             found = jnp.zeros((tile, rows), jnp.bfloat16)
             for m in range(per_owner):
@@ -333,12 +340,14 @@
                 return (
                     totals[0] + jnp.sum(raised, axis=0, keepdims=True),
                     totals[1] + jnp.sum(target * scores, axis=0, keepdims=True),
+                    totals[2] + jnp.sum(raised * scores, axis=0, keepdims=True),
                 )
 
             zero = jnp.zeros((1, rows), jnp.float32)
-            norm, dotted = lax.fori_loop(0, tiles, step, (zero, zero))
+            norm, dotted, spread = lax.fori_loop(0, tiles, step, (zero, zero, zero))
             stats[at, 0:1, :] += norm
             stats[at, 1:2, :] += dotted
+            stats[at, 2:3, :] += spread
 
     def accumulate(slots, first):
         for kind in range(2):
@@ -374,7 +383,7 @@
         elif index == 2 and way == 0:
             for copy in unit_copies:
                 copy.wait_recv()
-            for copy in raw_copies:
+            for copy in raw_copies + radius_copies:
                 copy.start()
             score(0, 0)
             accumulate((0,), True)
@@ -408,7 +417,16 @@
     stat_copies = rep_copies(4, lambda at: stats, lambda at: stats_in.at[at])
     for copy in stat_copies:
         copy.start()
-    accumulate((groups // 2,), False)
+    last_turned = [weight_ref[0, kind].T for kind in range(2)]
+
+    def accumulate_last(at):
+        span = pl.ds(pl.multiple_of(at * block, block), block)
+        for kind in range(2):
+            sums[at, kind] += jnp.dot(
+                last_turned[kind], docs_all[groups // 2, :, span], preferred_element_type=jnp.float32
+            )
+
+    accumulate_last(pair_cross)
 
     def pull_copy(at, source, landing, peer):
         return pltpu.make_async_remote_copy(
@@ -423,15 +441,19 @@
     pair_out[...] = sums[pair_cross].astype(jnp.bfloat16)
     pair_copy = pull_copy(0, pair_out, pair_in, pair)
     pair_copy.start()
+    for at in (cross, pair, rep_at):
+        accumulate_last(at)
     for copy in stat_copies:
         copy.wait_recv()
-    shares = []
+    shares, projections = [], []
     for at in range(reps):
         total = stats[at]
         for origin in range(others):
             total = total + stats_in[origin, at]
         stats_in[0, at] = total
         shares.append((pull_scale / total).T[:, 0:1])
+        projected = (total[2:3, :] / total[0:1, :] - total[1:2, :]) * (LOSS_SCALE / width)
+        projections.append(jnp.broadcast_to(projected, total.shape).T[:, 0:1])
     own_stats = stats_in[0, rep_at]
     loss_ref[...] = jnp.log(own_stats[0:1, :]) - own_stats[1:2, :]
     pair_copy.wait_recv()
@@ -455,40 +477,36 @@
         span = pl.ds(at * rows, rows)
         pull_ref[at] = sums[rep_at, 0, span, :] * shares[at] - sums[rep_at, 1, span, :]
     near_copy.wait_recv()
-    ones = jnp.ones((8, block), jnp.bfloat16)
+    for copy in radius_copies:
+        copy.wait_recv()
     own_cols = pl.ds(pl.multiple_of(rep_at * block, block), block)
+    group_terms = None
     for at in range(reps):
         held = pull_ref[at] + near_in[at].astype(jnp.float32)
+        unit = unit_all[at, :, own_cols].astype(jnp.float32)
         cross_copies[at].wait_recv()
         held = held + cross_in[at].astype(jnp.float32)
-        pull_ref[at] = held
-        unit = unit_all[at, :, own_cols].astype(jnp.float32)
-        project_out[at] = dot_nt(ones, (unit * held).astype(jnp.bfloat16))
-    project_copies = rep_copies(5, lambda at: project_out, lambda at: project_in.at[at])
-    for copy in project_copies:
-        copy.start()
-    for copy in radius_copies + project_copies:
-        copy.wait_recv()
-    for at in range(reps):
-        total = project_out[at]
-        for origin in range(others):
-            total = total + project_in[origin, at]
-        projection = (total * (1.0 / width)).T[:, 0:1]
-        unit = unit_all[at, :, own_cols].astype(jnp.float32)
-        grad_cols[at] = ((pull_ref[at] - unit * projection) / radius_all[at, :, 0:1]).astype(
+        grad_cols[at] = ((held - unit * projections[at]) / radius_all[at, :, 0:1]).astype(
             jnp.bfloat16
         )
-    grad_copies = rep_copies(6, lambda peer: grad_cols.at[peer], own_block(grad_home))
+        if at == reps // 2 - 1:
+            group_terms = jnp.dot(
+                raw_turned[:, 0 : all_rows // 2],
+                grad_cols[0 : reps // 2].reshape(all_rows // 2, block),
+                preferred_element_type=jnp.float32,
+            )
+    grad_copies = rep_copies(5, lambda peer: grad_cols.at[peer], own_block(grad_home))
     for copy in grad_copies:
         copy.start()
-    grad_home[rep_at] = grad_cols[rep_at]
-
     out_rows = width // groups
     parts = 2
     piece = block // parts
-    group_terms = jnp.dot(
-        raw_turned[...], grad_cols[...].reshape(all_rows, block), preferred_element_type=jnp.float32
-    ).astype(jnp.bfloat16).reshape(groups, out_rows, block)
+    group_terms += jnp.dot(
+        raw_turned[:, all_rows // 2 :],
+        grad_cols[reps // 2 :].reshape(all_rows // 2, block),
+        preferred_element_type=jnp.float32,
+    )
+    group_terms = group_terms.astype(jnp.bfloat16).reshape(groups, out_rows, block)
     for part in range(parts):
         terms_out[part] = group_terms[:, :, part * piece : (part + 1) * piece]
     far_first = sorted(range(1, groups), key=lambda step: abs(step - groups // 2))
@@ -506,6 +524,7 @@
             )
             copy.start()
             term_copies.append(copy)
+    grad_home[rep_at] = grad_cols[rep_at]
     for copy in grad_copies:
         copy.wait_recv()
     query_grad = dot_nt(grad_home[0], adapter_ref[:, 0:block])
@@ -543,7 +562,7 @@
             ring_copy(way, index).wait_send()
     for copy in (
         meta_copies + unit_copies + radius_copies + raw_copies + stat_copies
-        + [pair_copy, near_copy] + cross_copies + project_copies + grad_copies
+        + [pair_copy, near_copy] + cross_copies + grad_copies
         + term_copies + final_copies
     ):
         copy.wait_send()
@@ -566,10 +585,10 @@
             doc_rows.reshape(rows, candidates),
             labels.reshape(rows, candidates),
             routes,
-            jnp.zeros((rows, 8 - fanout), jnp.int32),
+            jnp.zeros((rows, 16 - fanout), jnp.int32),
         ],
         axis=1,
-    ).T
+    ).T.astype(jnp.bfloat16)
     bf16, f32 = jnp.bfloat16, jnp.float32
     vmem = pltpu.VMEM
     dma = pltpu.SemaphoreType.DMA
@@ -591,7 +610,7 @@
             vmem((groups, doc_count, width), bf16),
             vmem((reps, rows, width), bf16),
             vmem((reps, rows, width), bf16),
-            vmem((reps, 2 * candidates + 8, rows), jnp.int32),
+            vmem((reps, 2 * candidates + 16, rows), bf16),
             vmem((reps, rows, 128), f32),
             vmem((groups, doc_count, all_rows), bf16),
             vmem((doc_count, rows), bf16),
@@ -609,8 +628,6 @@
             vmem((reps, rows, block), bf16),
             vmem((reps, rows, block), bf16),
             vmem((reps, rows, block), f32),
-            vmem((reps, 8, rows), f32),
-            vmem((others, reps, 8, rows), f32),
             vmem((reps, rows, block), bf16),
             vmem((reps, rows, block), bf16),
             vmem((2, groups, out_rows, block // 2), bf16),
@@ -619,8 +636,8 @@
             dma((4,)),
             dma((2, groups - 1)),
             dma((2, groups - 1)),
-            dma((7, others)),
-            dma((7, others)),
+            dma((6, others)),
+            dma((6, others)),
             dma((2 + reps,)),
             dma((2 + reps,)),
             dma((2, groups - 1)),

time: 82.7 us -> 81 us (0.979)
  Pallas kernels: 79 us -> 75.8 us
  other arithmetic: 0.87 us -> 2.29 us
    pallas_call x1, Pallas kernels: 79 us -> 75.8 us  [gathered_on_device(): pl.pallas_call(functools.partial(gathered_kernel, groups, reps, fanout, p...]
    another operation x0 -> x3, other arithmetic: none -> 2.21 us
    transpose x1 -> x0, other arithmetic: 0.87 us -> none  [gathered_on_device(): meta = jnp.concatenate([doc_rows.reshape(rows, candidates), labels.reshap...]
where the time goes in v4:
time: 81 us; the launch traced here: 80.7 us
  Pallas kernels  75.8 us (94%)
  other arithmetic  2.29 us (3%)
  local copies, waits for them, and re-layouts  2 us (2%)
    pallas_call x1, Pallas kernels, gathered_on_device(): pl.pallas_call(functools.partial(gathered_kernel, groups, reps, fanout, p...  75.8 us
    another operation x3, other arithmetic  2.21 us
    unnamed x3, local copies, waits for them, and re-layouts  1.92 us

profile of v4, /device:TPU:0, one launch (start us, length us, event | category | flops | bytes accessed | tf_op | source)
XLA Modules:
  0.0 80.7 jit_solution(18370716050552352051)
XLA Ops:
  0.6 0.1 pad.3.clone
  0.7 0.7 convert.15
  1.4 0.8 convert.13
  2.2 0.8 convert.14
  2.9 0.1 maximum_bitcast_fusion.meta_hbm
  3.0 75.8 %shard_map.85 = (f32[1,128]{1,0:T(1,128)S(1)}, bf16[128,1024]{1,0:T(8,128)(2,1)S(1)}, bf16[128,1024]{1,0:T(8,128)(2,1)S(1)}) custom-call(bf16[128,1024]{1,0:T(8,128)(2,1)} %queries_ref.1, bf16[1024,1024]{1,0:T(8,128)(2,1)} %adapter_hbm.1, bf16[256,1024]{1,0:T(8,128)(2,1)} %doc_hbm.1, bf16[144,128]{1,0:T(8,128)(2,1)S(1)} %maximum_bitcast_fusion.meta_hbm), custom_call_target="tpu_custom_call" | custom-call | tf_op jit(solution)/shard_map/pallas_call | solution.py:595
  78.8 0.5 copy.12
  79.3 0.7 copy.13
  80.0 0.7 copy.14
  (1 shorter events, 0.0 us)

commit v5 on v4

--- a/solution.py
+++ b/solution.py
@@ -168,11 +168,11 @@
     groups, reps, fanout, per_owner, inverse_root,
     queries_ref, adapter_hbm, doc_hbm, meta_hbm,
     loss_ref, query_grad_ref, adapter_grad_ref,
-    adapter_ref, doc_ref, docs_all, unit_all, raw_all, meta_all, radius_all,
+    adapter_ref, doc_ref, docs_all, unit_all, raw_all, meta_ref, meta_all, radius_all,
     marks_all, here_ref, raw_turned, score_ref, weight_ref, sums, label_sum, stats, stats_in,
     pair_out, pair_in, cross_out, cross_in, near_out, near_in, pull_ref,
     grad_cols, grad_home,
-    terms_out, terms_in, final_cols,
+    terms_out, travel_out, travel_in, final_cols,
     load_sem, ring_send, ring_recv, rep_send, rep_recv, pull_send, pull_recv,
     terms_send, terms_recv, final_send, final_recv,
 ):
@@ -195,7 +195,7 @@
                 (doc_hbm, doc_ref),
                 (queries_ref, raw_all.at[rep_at]),
                 (adapter_hbm, adapter_ref),
-                (meta_hbm, meta_all.at[rep_at]),
+                (meta_hbm, meta_ref),
             )
         )
     ]
@@ -266,6 +266,7 @@
         return lambda at: ref.at[rep_at]
 
     loads[3].wait()
+    meta_all[rep_at] = meta_ref[...].astype(jnp.float32).astype(jnp.bfloat16)
     meta_copies = rep_copies(0, own_block(meta_all), own_block(meta_all))
     for copy in meta_copies:
         copy.start()
@@ -509,35 +510,51 @@
     group_terms = group_terms.astype(jnp.bfloat16).reshape(groups, out_rows, block)
     for part in range(parts):
         terms_out[part] = group_terms[:, :, part * piece : (part + 1) * piece]
-    far_first = sorted(range(1, groups), key=lambda step: abs(step - groups // 2))
+    hops = groups // 2
+
+    def term_copy(way, part, step):
+        return pltpu.make_async_remote_copy(
+            src_ref=travel_out.at[way, part, step],
+            dst_ref=travel_in.at[way, part, step],
+            send_sem=terms_send.at[way, part, step],
+            recv_sem=terms_recv.at[way, part, step],
+            device_id=(right if way == 0 else left, rep_at),
+            device_id_type=MESH,
+        )
+
     term_copies = []
-    for part in range(parts):
-        for step in far_first:
-            peer = lax.rem(docs_at + step, groups)
-            copy = pltpu.make_async_remote_copy(
-                src_ref=terms_out.at[part, peer],
-                dst_ref=terms_in.at[part, step - 1],
-                send_sem=terms_send.at[part, step - 1],
-                recv_sem=terms_recv.at[part, step - 1],
-                device_id=(peer, rep_at),
-                device_id_type=MESH,
-            )
+    for step in range(hops):
+        distance = hops - step
+        for part, way in ((0, 0), (1, 1), (1, 0), (0, 1)):
+            start = 0 if part == way else 1
+            if step < start:
+                continue
+            ahead = distance if way == 0 else groups - distance
+            target = ring_group(lax.rem(place + ahead, groups), groups)
+            running = terms_out[part, target]
+            if step > start:
+                term_copy(way, part, step - 1).wait_recv()
+                running = (
+                    running.astype(jnp.float32) + travel_in[way, part, step - 1].astype(jnp.float32)
+                ).astype(jnp.bfloat16)
+            travel_out[way, part, step] = running
+            copy = term_copy(way, part, step)
             copy.start()
             term_copies.append(copy)
-    grad_home[rep_at] = grad_cols[rep_at]
-    for copy in grad_copies:
-        copy.wait_recv()
-    query_grad = dot_nt(grad_home[0], adapter_ref[:, 0:block])
-    for at in range(1, reps):
-        query_grad += dot_nt(grad_home[at], adapter_ref[:, at * block : (at + 1) * block])
-    query_grad_ref[...] = query_grad.astype(jnp.bfloat16)
+        if step == hops - 2:
+            grad_home[rep_at] = grad_cols[rep_at]
+            for copy in grad_copies:
+                copy.wait_recv()
+            query_grad = dot_nt(grad_home[0], adapter_ref[:, 0:block])
+            for at in range(1, reps):
+                query_grad += dot_nt(grad_home[at], adapter_ref[:, at * block : (at + 1) * block])
+            query_grad_ref[...] = query_grad.astype(jnp.bfloat16)
     final_copies = []
     for part in range(parts):
         summed = terms_out[part, docs_at].astype(jnp.float32)
-        for at in range(groups - 1):
-            term_copies[part * (groups - 1) + at].wait_recv()
-        for at in range(groups - 1):
-            summed = summed + terms_in[part, at].astype(jnp.float32)
+        for way in range(2):
+            term_copy(way, part, hops - 1).wait_recv()
+            summed = summed + travel_in[way, part, hops - 1].astype(jnp.float32)
         final_cols[part, rep_at] = (summed * inverse_root).astype(jnp.bfloat16)
         for at in range(others):
             copy = pltpu.make_async_remote_copy(
@@ -588,7 +605,7 @@
             jnp.zeros((rows, 16 - fanout), jnp.int32),
         ],
         axis=1,
-    ).T.astype(jnp.bfloat16)
+    ).T
     bf16, f32 = jnp.bfloat16, jnp.float32
     vmem = pltpu.VMEM
     dma = pltpu.SemaphoreType.DMA
@@ -610,6 +627,7 @@
             vmem((groups, doc_count, width), bf16),
             vmem((reps, rows, width), bf16),
             vmem((reps, rows, width), bf16),
+            vmem((2 * candidates + 16, rows), jnp.int32),
             vmem((reps, 2 * candidates + 16, rows), bf16),
             vmem((reps, rows, 128), f32),
             vmem((groups, doc_count, all_rows), bf16),
@@ -631,7 +649,8 @@
             vmem((reps, rows, block), bf16),
             vmem((reps, rows, block), bf16),
             vmem((2, groups, out_rows, block // 2), bf16),
-            vmem((2, groups - 1, out_rows, block // 2), bf16),
+            vmem((2, 2, groups // 2, out_rows, block // 2), bf16),
+            vmem((2, 2, groups // 2, out_rows, block // 2), bf16),
             vmem((2, reps, out_rows, block // 2), bf16),
             dma((4,)),
             dma((2, groups - 1)),
@@ -640,8 +659,8 @@
             dma((6, others)),
             dma((2 + reps,)),
             dma((2 + reps,)),
-            dma((2, groups - 1)),
-            dma((2, groups - 1)),
+            dma((2, 2, groups // 2)),
+            dma((2, 2, groups // 2)),
             dma((2, others)),
             dma((2, others)),
         ],

time: 81 us -> 80.8 us (level)
  other arithmetic: 2.29 us -> 0.87 us
  Pallas kernels: 75.8 us -> 77 us
    another operation x3 -> x0, other arithmetic: 2.21 us -> none
    pallas_call x1, Pallas kernels: 75.8 us -> 77 us  [gathered_on_device(): pl.pallas_call(functools.partial(gathered_kernel, groups, reps, fanout, p...]
    transpose x0 -> x1, other arithmetic: none -> 0.87 us  [gathered_on_device(): meta = jnp.concatenate([doc_rows.reshape(rows, candidates), labels.reshap...]
where the time goes in v5:
time: 80.8 us; the launch traced here: 80.6 us
  Pallas kernels  77 us (95%)
  local copies, waits for them, and re-layouts  1.99 us (2%)
  other arithmetic  0.87 us (1%)
    pallas_call x1, Pallas kernels, gathered_on_device(): pl.pallas_call(functools.partial(gathered_kernel, groups, reps, fanout, p...  77 us
    unnamed x3, local copies, waits for them, and re-layouts  1.92 us

profile of v5, /device:TPU:0, one launch (start us, length us, event | category | flops | bytes accessed | tf_op | source)
XLA Modules:
  0.0 80.6 jit_solution(2785661596482409729)
XLA Ops:
  0.6 0.1 pad.3.clone
  0.7 0.9 %add_bitcast_fusion.meta_hbm = s32[144,128]{1,0:T(8,128)S(1)} fusion(s32[128,4]{0,1:T(4,128)} %param.9, s32[128,64]{0,1:T(8,128)} %bitcast.6, s32[128,64]{0,1:T(8,128)} %bitcast.7, s32[144]{0:T(256)S(1)} %pad.3.clone), kind=kLoop, calls=%fused_computation | loop fusion | flops 55296 | bytes 141888 | tf_op jit(solution)/shard_map/transpose | solution.py:608
  1.6 77.0 %shard_map.85 = (f32[1,128]{1,0:T(1,128)S(1)}, bf16[128,1024]{1,0:T(8,128)(2,1)S(1)}, bf16[128,1024]{1,0:T(8,128)(2,1)S(1)}) custom-call(bf16[128,1024]{1,0:T(8,128)(2,1)} %queries_ref.1, bf16[1024,1024]{1,0:T(8,128)(2,1)} %adapter_hbm.1, bf16[256,1024]{1,0:T(8,128)(2,1)} %doc_hbm.1, s32[144,128]{1,0:T(8,128)S(1)} %add_bitcast_fusion.meta_hbm), custom_call_target="tpu_custom_call" | custom-call | tf_op jit(solution)/shard_map/pallas_call | solution.py:612
  78.6 0.5 copy.12
  79.1 0.7 copy.13
  79.9 0.7 copy.14
  (1 shorter events, 0.0 us)

commit v6 on v4

--- a/solution.py
+++ b/solution.py
@@ -168,7 +168,7 @@
     groups, reps, fanout, per_owner, inverse_root,
     queries_ref, adapter_hbm, doc_hbm, meta_hbm,
     loss_ref, query_grad_ref, adapter_grad_ref,
-    adapter_ref, doc_ref, docs_all, unit_all, raw_all, meta_all, radius_all,
+    adapter_ref, doc_ref, docs_all, unit_all, raw_all, meta_ref, meta_all, radius_all,
     marks_all, here_ref, raw_turned, score_ref, weight_ref, sums, label_sum, stats, stats_in,
     pair_out, pair_in, cross_out, cross_in, near_out, near_in, pull_ref,
     grad_cols, grad_home,
@@ -195,7 +195,7 @@
                 (doc_hbm, doc_ref),
                 (queries_ref, raw_all.at[rep_at]),
                 (adapter_hbm, adapter_ref),
-                (meta_hbm, meta_all.at[rep_at]),
+                (meta_hbm, meta_ref),
             )
         )
     ]
@@ -266,6 +266,7 @@
         return lambda at: ref.at[rep_at]
 
     loads[3].wait()
+    meta_all[rep_at] = meta_ref[...].astype(jnp.float32).astype(jnp.bfloat16)
     meta_copies = rep_copies(0, own_block(meta_all), own_block(meta_all))
     for copy in meta_copies:
         copy.start()
@@ -588,7 +589,7 @@
             jnp.zeros((rows, 16 - fanout), jnp.int32),
         ],
         axis=1,
-    ).T.astype(jnp.bfloat16)
+    ).T
     bf16, f32 = jnp.bfloat16, jnp.float32
     vmem = pltpu.VMEM
     dma = pltpu.SemaphoreType.DMA
@@ -610,6 +611,7 @@
             vmem((groups, doc_count, width), bf16),
             vmem((reps, rows, width), bf16),
             vmem((reps, rows, width), bf16),
+            vmem((2 * candidates + 16, rows), jnp.int32),
             vmem((reps, 2 * candidates + 16, rows), bf16),
             vmem((reps, rows, 128), f32),
             vmem((groups, doc_count, all_rows), bf16),

time: 81 us -> 79.6 us (0.983)
  other arithmetic: 2.29 us -> 0.87 us
    another operation x3 -> x0, other arithmetic: 2.21 us -> none
    transpose x0 -> x1, other arithmetic: none -> 0.87 us  [gathered_on_device(): meta = jnp.concatenate([doc_rows.reshape(rows, candidates), labels.reshap...]
where the time goes in v6:
time: 79.6 us; the launch traced here: 79.4 us
  Pallas kernels  75.8 us (95%)
  local copies, waits for them, and re-layouts  1.99 us (2%)
  other arithmetic  0.87 us (1%)
    pallas_call x1, Pallas kernels, gathered_on_device(): pl.pallas_call(functools.partial(gathered_kernel, groups, reps, fanout, p...  75.8 us
    unnamed x3, local copies, waits for them, and re-layouts  1.92 us

profile of v6, /device:TPU:0, one launch (start us, length us, event | category | flops | bytes accessed | tf_op | source)
XLA Modules:
  0.0 79.4 jit_solution(3914290013643141506)
XLA Ops:
  0.6 0.1 pad.3.clone
  0.7 0.9 %add_bitcast_fusion.meta_hbm = s32[144,128]{1,0:T(8,128)S(1)} fusion(s32[128,4]{0,1:T(4,128)} %param.9, s32[128,64]{0,1:T(8,128)} %bitcast.6, s32[128,64]{0,1:T(8,128)} %bitcast.7, s32[144]{0:T(256)S(1)} %pad.3.clone), kind=kLoop, calls=%fused_computation | loop fusion | flops 55296 | bytes 141888 | tf_op jit(solution)/shard_map/transpose | solution.py:592
  1.6 75.8 %shard_map.85 = (f32[1,128]{1,0:T(1,128)S(1)}, bf16[128,1024]{1,0:T(8,128)(2,1)S(1)}, bf16[128,1024]{1,0:T(8,128)(2,1)S(1)}) custom-call(bf16[128,1024]{1,0:T(8,128)(2,1)} %queries_ref.1, bf16[1024,1024]{1,0:T(8,128)(2,1)} %adapter_hbm.1, bf16[256,1024]{1,0:T(8,128)(2,1)} %doc_hbm.1, s32[144,128]{1,0:T(8,128)S(1)} %add_bitcast_fusion.meta_hbm), custom_call_target="tpu_custom_call" | custom-call | tf_op jit(solution)/shard_map/pallas_call | solution.py:596
  77.4 0.5 copy.12
  77.9 0.7 copy.13
  78.6 0.7 copy.14
  (1 shorter events, 0.0 us)
